TPU v7x, 128 devices: a whole 4x4x4 slice. The times are simulated.
128 devices in a mesh: req: 16 (over z, x), head: 8 (over y, core).
Axes of the slice: x: 4, y: 4, z: 4, core: 2. Of those that a mesh axis runs over, the one named last changes fastest.
Arguments:
- embedded: bfloat16 [2, 96, 8192], P(None, None, 'req'), may hold values from -6 to 6
- ssm_states: bfloat16 [2, 192, 128, 128, 128], P(None, 'req', 'head'), may hold values from -0.59765625 to 0.59765625
- conv_tail_x: bfloat16 [2, 192, 3, 16384], P(None, 'req', None, 'head'), may hold values from -6 to 6
- conv_tail_bc: bfloat16 [2, 192, 3, 2048], P(None, 'req', None, 'head'), may hold values from -6 to 6
- prefill_slot: int32 [96], replicated, may hold values from 0 to 191, as said below
- decode_slot: int32 [96], replicated, may hold values from 0 to 95, as said below
- norm_gain: float32 [2, 8192], P(None, 'req'), may hold values from 0.5 to 1.5
- w_gate: bfloat16 [2, 8192, 16384], P(None, 'req', 'head'), may hold values from -0.0625 to 0.0625
- w_input: bfloat16 [2, 8192, 16384], P(None, 'req', 'head'), may hold values from -0.0625 to 0.0625
- w_groups: bfloat16 [2, 8192, 2048], P(None, 'req', 'head'), may hold values from -0.0625 to 0.0625
- w_step: bfloat16 [2, 8192, 128], P(None, 'req', 'head'), may hold values from -0.0625 to 0.0625
- conv_input: float32 [2, 4, 16384], P(None, None, 'head'), may hold values from -3 to 3
- conv_groups: float32 [2, 4, 2048], P(None, None, 'head'), may hold values from -3 to 3
- step_bias: float32 [2, 128], P(None, 'head'), may hold values from -3 to 0
- decay_rate: float32 [2, 128], P(None, 'head'), may hold values from 0.05 to 5
- skip_gain: float32 [2, 128], P(None, 'head'), may hold values from 0.5 to 1.5
- out_gain: float32 [2, 16384], P(None, 'head'), may hold values from 0.5 to 1.5
- w_output: bfloat16 [2, 16384, 8192], P(None, 'head', 'req'), may hold values from -0.046875 to 0.046875
Outputs:
- decoded: bfloat16 [2, 96, 8192], P(None, None, 'req')
Inputs may be any that keep to these rules, and one draw needn't show every extreme that they name: `prefill_slot`: distinct slots; the slots of prefill owner q are q * 12 to q * 12 + 11, and some owner has all 12 slots used. No two requests with the same prefill owner have the same decode owner (decode_slot // 6). `decode_slot`: A permutation of the requests' rows.
All inputs are finite; a program needn't handle non-finite values.
Results may differ from a plain program's by a relative error of at most 0.008.
Values may be sent and summed in bfloat16 or wider, within the bound.
A program may use at most 256 MiB of HBM per device.

v0:
```python
import jax
import jax.numpy as jnp
from jax import lax
from jax.sharding import PartitionSpec as P

D = 8192
P_SIZE = 128
N = 128
G = 8
DI = 16384
HG = 16


epsilon = 1e-05


def ssm_rows(x_pre, bc_pre, dt_pre, states, tails_x, tails_bc, conv_in, conv_grp, bias, rate, skip):
    seq_x = jnp.concatenate([tails_x.astype(jnp.float32), x_pre[:, None, :]], axis=1)
    x_conv = jax.nn.silu(jnp.sum(seq_x * conv_in[None], axis=1))
    seq_bc = jnp.concatenate([tails_bc.astype(jnp.float32), bc_pre[:, None, :]], axis=1)
    bc_conv = jax.nn.silu(jnp.sum(seq_bc * conv_grp[None], axis=1))
    new_tx = jnp.concatenate([tails_x[:, 1:], x_pre.astype(jnp.bfloat16)[:, None, :]], axis=1)
    new_tbc = jnp.concatenate([tails_bc[:, 1:], bc_pre.astype(jnp.bfloat16)[:, None, :]], axis=1)
    rows = x_pre.shape[0]
    heads = dt_pre.shape[1]
    groups = bc_conv.shape[1] // (2 * N)
    pairs = bc_conv.reshape(rows, groups, 2 * N)
    b_head = jnp.repeat(pairs[:, :, :N], HG, axis=1)
    c_head = jnp.repeat(pairs[:, :, N:], HG, axis=1)
    delta = jax.nn.softplus(dt_pre + bias[None, :])
    decay = jnp.exp(-delta * rate[None, :])
    x_heads = x_conv.reshape(rows, heads, P_SIZE)
    new_states = (
        decay[:, :, None, None] * states
        + (delta[:, :, None] * x_heads)[:, :, :, None] * b_head[:, :, None, :]
    )
    result = jnp.einsum("rhpn,rhn->rhp", new_states, c_head, precision=lax.Precision.HIGHEST)
    result = result + skip[None, :, None] * x_heads
    return (result.reshape(rows, heads * P_SIZE), new_states, new_tx, new_tbc)


def gate_norm(ssm_out, gate_pre, gain):
    rows = ssm_out.shape[0]
    gated = ssm_out * jax.nn.silu(gate_pre)
    grouped = gated.reshape(rows, -1, DI // G)
    mean_sq = jnp.mean(grouped * grouped, axis=2, keepdims=True)
    normed = (grouped * lax.rsqrt(mean_sq + epsilon)).reshape(rows, -1) * gain[None, :]
    return normed.astype(jnp.bfloat16)


def pick_slots(block, slots, live_rows, axis):
    picked = jnp.take(block, slots, axis=axis)
    mask_shape = [slots.shape[0] if dim_idx == axis else 1 for dim_idx in range(picked.ndim)]
    return jnp.where(live_rows.reshape(mask_shape), picked, jnp.zeros((), block.dtype))


def on_device(
    embedded,
    ssm_states,
    conv_tail_x,
    conv_tail_bc,
    prefill_slot,
    decode_slot,
    norm_gain,
    w_gate,
    w_input,
    w_groups,
    w_step,
    conv_input,
    conv_groups,
    step_bias,
    decay_rate,
    skip_gain,
    out_gain,
    w_output,
):
    steps = embedded.shape[0]
    total_rows = embedded.shape[1]
    layers = ssm_states.shape[0]
    capacity = ssm_states.shape[1]
    dev_count = lax.axis_size("req")
    per_dev = total_rows // dev_count
    own_index = lax.axis_index("req")
    row_ids = jnp.arange(total_rows, dtype=jnp.int32)
    hits = decode_slot[:, None] == row_ids[None, :]
    row_slot = jnp.sum(jnp.where(hits, prefill_slot[:, None], 0), axis=0)
    row_source = row_slot // capacity
    row_local = row_slot % capacity
    own_sources = lax.dynamic_slice_in_dim(row_source, own_index * per_dev, per_dev)
    from_here = row_source.reshape(dev_count, per_dev) == own_index
    send_slot = jnp.sum(jnp.where(from_here, row_local.reshape(dev_count, per_dev), 0), axis=1)
    send_live = jnp.any(from_here, axis=1)
    held = [None] * layers
    arrived = (
        lax.all_to_all(
            pick_slots(ssm_states, send_slot, send_live, 1),
            "req",
            split_axis=1,
            concat_axis=1,
            tiled=True,
        ),
        lax.all_to_all(
            pick_slots(conv_tail_x, send_slot, send_live, 1),
            "req",
            split_axis=1,
            concat_axis=1,
            tiled=True,
        ),
        lax.all_to_all(
            pick_slots(conv_tail_bc, send_slot, send_live, 1),
            "req",
            split_axis=1,
            concat_axis=1,
            tiled=True,
        ),
    )
    for layer_idx in range(layers):
        held[layer_idx] = (
            jnp.take(arrived[0][layer_idx], own_sources, axis=0).astype(jnp.float32),
            jnp.take(arrived[1][layer_idx], own_sources, axis=0),
            jnp.take(arrived[2][layer_idx], own_sources, axis=0),
        )
    streams = [embedded[step_idx].astype(jnp.float32) for step_idx in range(steps)]
    for layer_idx in range(layers):
        weight_out = w_output[layer_idx]
        for step_idx in range(steps):
            stream = streams[step_idx]
            squares = lax.psum(jnp.sum(stream * stream, axis=1), "req")
            normed = (
                stream * lax.rsqrt(squares / D + epsilon)[:, None] * norm_gain[layer_idx][None, :]
            ).astype(jnp.bfloat16)
            gate_pre, x_pre, bc_pre, dt_pre = (
                lax.psum_scatter(
                    jnp.dot(normed, w_gate[layer_idx], preferred_element_type=jnp.float32),
                    "req",
                    scatter_dimension=0,
                    tiled=True,
                ),
                lax.psum_scatter(
                    jnp.dot(normed, w_input[layer_idx], preferred_element_type=jnp.float32),
                    "req",
                    scatter_dimension=0,
                    tiled=True,
                ),
                lax.psum_scatter(
                    jnp.dot(normed, w_groups[layer_idx], preferred_element_type=jnp.float32),
                    "req",
                    scatter_dimension=0,
                    tiled=True,
                ),
                lax.psum_scatter(
                    jnp.dot(normed, w_step[layer_idx], preferred_element_type=jnp.float32),
                    "req",
                    scatter_dimension=0,
                    tiled=True,
                ),
            )
            cached, tails_x, tails_bc = held[layer_idx]
            ssm_out, cached, tails_x, tails_bc = ssm_rows(
                x_pre,
                bc_pre,
                dt_pre,
                cached,
                tails_x,
                tails_bc,
                conv_input[layer_idx],
                conv_groups[layer_idx],
                step_bias[layer_idx],
                decay_rate[layer_idx],
                skip_gain[layer_idx],
            )
            held[layer_idx] = (cached, tails_x, tails_bc)
            normed_out = gate_norm(ssm_out, gate_pre, out_gain[layer_idx])
            partial_out = jnp.dot(
                lax.all_gather(normed_out, "req", axis=0, tiled=True),
                weight_out,
                preferred_element_type=jnp.float32,
            )
            streams[step_idx] = stream + lax.psum(partial_out, "head")
    return jnp.stack([item.astype(jnp.bfloat16) for item in streams])


def solution(mesh):
    return jax.shard_map(
        on_device,
        mesh=mesh,
        in_specs=(
            P(None, None, "req"),
            P(None, "req", "head", None, None),
            P(None, "req", None, "head"),
            P(None, "req", None, "head"),
            P(),
            P(),
            P(None, "req"),
            P(None, "req", "head"),
            P(None, "req", "head"),
            P(None, "req", "head"),
            P(None, "req", "head"),
            P(None, None, "head"),
            P(None, None, "head"),
            P(None, "head"),
            P(None, "head"),
            P(None, "head"),
            P(None, "head"),
            P(None, "head", "req"),
        ),
        out_specs=P(None, None, "req"),
        check_vma=False,
    )
```

profile of v0, /device:TPU:1, one launch (start us, length us, event | category | flops | bytes accessed | tf_op | source)
XLA Modules:
  0.0 905.7 jit_solution(9008200150749559157)
XLA Ops:
  10.1 8.4 all-to-all-start.2
  21.1 11.7 %gather_fusion = bf16[16,2,16,128,128]{4,3,2,1,0:T(8,128)(2,1)} fusion(bf16[2,12,16,128,128]{4,3,2,1,0:T(8,128)(2,1)} %param.25, s32[1024]{0:T(1024)S(1)} %pad_clamp_fusion.1), kind=kCustom, calls=%fused_computation.6 | custom fusion | bytes 33554496 | tf_op jit(solution)/shard_map/jit(_take)/gather | solution.py:52
  32.8 6.7 all-to-all-start.1
  39.5 14.3 %select_bitcast_fusion = bf16[2,16,16,128,128]{4,3,2,0,1:T(8,128)(2,1)} fusion(bf16[16,2,16,128,128]{4,3,2,1,0:T(8,128)(2,1)} %gather_fusion, pred[16]{0:T(512)(128)(4,1)S(1)} %get-tuple-element.80, pred[16]{0:T(512)(128)(4,1)S(1)} %compare_and_fusion.1), kind=kLoop, calls=%fused_computation.9 | loop fusion | flops 16777216 | bytes 33554464 | tf_op jit(solution)/shard_map/jit(_where)/select_n | solution.py:54
  53.8 6.8 all-to-all-start
  60.8 265.4 %all-reduce.19 = (f32[96]{0:T(128)S(1)}, f32[96]{0:T(128)S(1)}) all-reduce(f32[96]{0:T(128)S(1)} %get-tuple-element.10, f32[96]{0:T(128)S(1)} %get-tuple-element.11), channel_id=1, replica_groups=mesh['req'=16,'head'=8] {'req'}, use_global_device_ids=true, to_apply=%region_1.2 | all-reduce | flops 192 | bytes 1536 | tf_op jit(solution)/shard_map/psum | solution.py:128
  328.0 3.0 fusion.44
  331.0 3.0 fusion.46
  338.9 58.6 %all-reduce.18 = (f32[96,16]{1,0:T(8,128)S(1)}, f32[96,16]{1,0:T(8,128)S(1)}) all-reduce(f32[96,16]{1,0:T(8,128)S(1)} %fusion.122, f32[96,16]{1,0:T(8,128)S(1)} %fusion.120), channel_id=2, replica_groups=mesh['req'=16,'head'=8] {'req'}, use_global_device_ids=true, to_apply=%region_2.3.clone | all-reduce | flops 3072 | bytes 24576
  401.6 38.4 %all-reduce.31.cloned.1.call-done = (f32[96,256]{1,0:T(8,128)}, f32[96,256]{1,0:T(8,128)}, f32[96,2048]{1,0:T(8,128)}, f32[96,2048]{1,0:T(8,128)}, f32[96,2048]{1,0:T(8,128)}, /*index=5*/f32[96,2048]{1,0:T(8,128)}) async-done(((f32[96,256]{1,0:T(8,128)}, f32[96,256]{1,0:T(8,128)}, f32[96,2048]{1,0:T(8,128)}, f32[96,2048]{1,0:T(8,128)}, f32[96,2048]{1,0:T(8,128)}, /*index=5*/f32[96,2048]{1,0:T(8,128)}), ...) | async-done | bytes 3342352
  444.3 21.9 %slice_bitcast_fusion = (bf16[16,16,128,128]{3,2,1,0:T(8,128)(2,1)}, bf16[16,16,128,128]{3,2,1,0:T(8,128)(2,1)}) fusion(bf16[2,16,16,128,128]{4,3,2,0,1:T(8,128)(2,1)} %all-to-all-done), kind=kLoop, calls=%fused_computation.10 | loop fusion | bytes 33554432 | tf_op jit(solution)/shard_map/squeeze | solution.py:119
  466.2 6.1 gather_fusion.3
  472.3 12.5 %fusion.9 = f32[6,16,1,128]{3,2,1,0:T(1,128)S(1)} fusion(f32[6,16,128,1]{2,3,1,0:T(1,128)S(1)} %bitcast.351, f32[6,128]{1,0:T(8,128)S(1)} %get-tuple-element.108, f32[6,16,128]{2,1,0:T(8,128)S(1)} %broadcast_multiply_fusion.3, f32[6,16]{1,0:T(8,128)S(1)} %get-tuple-element.120, bf16[6,16,128,128]{3,2,1,0:T(8,128)(2,1)} %gather_fusion.3, ...), kind=kOutput, calls=%fused_computation.23 | convolution fusion | flops 26738688 | bytes 3296646 | tf_op jit(solution)/shard_map/rhpn,rhn->rhp/dot_general | solution.py:37
  484.8 12.7 %fusion.4 = f32[6,16,1,128]{3,2,1,0:T(1,128)S(1)} fusion(f32[6,16,128,1]{2,3,1,0:T(1,128)S(1)} %bitcast.349, f32[6,128]{1,0:T(8,128)S(1)} %get-tuple-element.106, f32[6,16,128]{2,1,0:T(8,128)S(1)} %broadcast_multiply_fusion.1, f32[6,16]{1,0:T(8,128)S(1)} %get-tuple-element.62, f32[6,128]{1,0:T(8,128)S(1)} %get-tuple-element.108, ...), kind=kOutput, calls=%fused_computation.16 | convolution fusion | flops 31457280 | bytes 3349254 | tf_op jit(solution)/shard_map/rhpn,rhn->rhp/dot_general | solution.py:37
  499.9 18.2 %all-gather.2 = bf16[16,6,2048]{2,1,0:T(8,128)(2,1)S(1)} all-gather(bf16[1,6,2048]{2,1,0:T(8,128)(2,1)S(1)} %get-tuple-element.104), channel_id=1, replica_groups=mesh['req'=16,'head'=8] {'req'}, dimensions={0}, use_global_device_ids=true | all-gather | bytes 417792 | tf_op jit(solution)/shard_map/all_gather | solution.py:175
  518.2 17.1 %all-gather = bf16[16,6,2048]{2,1,0:T(8,128)(2,1)S(1)} all-gather(bf16[1,6,2048]{2,1,0:T(8,128)(2,1)S(1)} %get-tuple-element.105), channel_id=1, replica_groups=mesh['req'=16,'head'=8] {'req'}, dimensions={0}, use_global_device_ids=true | all-gather | bytes 417792 | tf_op jit(solution)/shard_map/all_gather | solution.py:175
  535.5 2.8 fusion.40
  538.2 2.7 fusion.42
  541.0 67.9 %all-reduce.35.cloned.1.call-done = (f32[96,512]{1,0:T(8,128)}, f32[96,512]{1,0:T(8,128)}) async-done(((f32[96,512]{1,0:T(8,128)}, f32[96,512]{1,0:T(8,128)}), (f32[96,512]{1,0:T(8,128)}, f32[96,512]{1,0:T(8,128)})) %all-reduce.35.cloned.1.call-update) | async-done | bytes 393232 | tf_op jit(solution)/shard_map/psum | solution.py:179
  610.1 33.5 %all-reduce.17 = (f32[96]{0:T(128)S(1)}, f32[96]{0:T(128)S(1)}) all-reduce(f32[96]{0:T(128)S(1)} %get-tuple-element.6, f32[96]{0:T(128)S(1)} %get-tuple-element.8), channel_id=1, replica_groups=mesh['req'=16,'head'=8] {'req'}, use_global_device_ids=true, to_apply=%region_14.18 | all-reduce | flops 192 | bytes 1536 | tf_op jit(solution)/shard_map/psum | solution.py:128
  644.9 3.2 fusion.32
  648.1 2.9 fusion.36
  655.7 6.1 gather_fusion.6
  662.0 58.0 %all-reduce.16 = (f32[96,16]{1,0:T(8,128)S(1)}, f32[96,16]{1,0:T(8,128)S(1)}) all-reduce(f32[96,16]{1,0:T(8,128)S(1)} %fusion.116, f32[96,16]{1,0:T(8,128)S(1)} %fusion.118), channel_id=14, replica_groups=mesh['req'=16,'head'=8] {'req'}, use_global_device_ids=true, to_apply=%region_35.39.clone | all-reduce | flops 3072 | bytes 24576
  720.1 36.0 %all-reduce.29.cloned.1.call-done = (f32[96,256]{1,0:T(8,128)}, f32[96,256]{1,0:T(8,128)}, f32[96,2048]{1,0:T(8,128)}, f32[96,2048]{1,0:T(8,128)}, f32[96,2048]{1,0:T(8,128)}, /*index=5*/f32[96,2048]{1,0:T(8,128)}) async-done(((f32[96,256]{1,0:T(8,128)}, f32[96,256]{1,0:T(8,128)}, f32[96,2048]{1,0:T(8,128)}, f32[96,2048]{1,0:T(8,128)}, f32[96,2048]{1,0:T(8,128)}, /*index=5*/f32[96,2048]{1,0:T(8,128)}), ...) | async-done | bytes 3342352
  760.4 12.5 %fusion.8 = f32[6,16,1,128]{3,2,1,0:T(1,128)S(1)} fusion(f32[6,16,128,1]{2,3,1,0:T(1,128)S(1)} %bitcast.352, f32[6,128]{1,0:T(8,128)S(1)} %get-tuple-element.99, f32[6,16,128]{2,1,0:T(8,128)S(1)} %broadcast_multiply_fusion.2, f32[6,16]{1,0:T(8,128)S(1)} %get-tuple-element.48, bf16[6,16,128,128]{3,2,1,0:T(8,128)(2,1)} %gather_fusion.6, ...), kind=kOutput, calls=%fused_computation.21 | convolution fusion | flops 26738688 | bytes 3296646 | tf_op jit(solution)/shard_map/rhpn,rhn->rhp/dot_general | solution.py:37
  772.9 12.7 %fusion = f32[6,16,1,128]{3,2,1,0:T(1,128)S(1)} fusion(f32[6,16,128,1]{2,3,1,0:T(1,128)S(1)} %bitcast.350, f32[6,128]{1,0:T(8,128)S(1)} %get-tuple-element.100, f32[6,16,128]{2,1,0:T(8,128)S(1)} %broadcast_multiply_fusion, f32[6,16]{1,0:T(8,128)S(1)} %get-tuple-element.114, f32[6,128]{1,0:T(8,128)S(1)} %get-tuple-element.99, ...), kind=kOutput, calls=%fused_computation.12 | convolution fusion | flops 31457280 | bytes 3349254 | tf_op jit(solution)/shard_map/rhpn,rhn->rhp/dot_general | solution.py:37
  788.0 18.2 %all-gather.3 = bf16[16,6,2048]{2,1,0:T(8,128)(2,1)S(1)} all-gather(bf16[1,6,2048]{2,1,0:T(8,128)(2,1)S(1)} %get-tuple-element.97), channel_id=1, replica_groups=mesh['req'=16,'head'=8] {'req'}, dimensions={0}, use_global_device_ids=true | all-gather | bytes 417792 | tf_op jit(solution)/shard_map/all_gather | solution.py:175
  806.4 2.8 fusion.28
  809.2 16.9 %all-gather.1 = bf16[16,6,2048]{2,1,0:T(8,128)(2,1)S(1)} all-gather(bf16[1,6,2048]{2,1,0:T(8,128)(2,1)S(1)} %get-tuple-element.96), channel_id=1, replica_groups=mesh['req'=16,'head'=8] {'req'}, dimensions={0}, use_global_device_ids=true | all-gather | bytes 417792 | tf_op jit(solution)/shard_map/all_gather | solution.py:175
  826.2 2.7 fusion.30
  829.0 68.0 %all-reduce.33.cloned.1.call-done = (f32[96,512]{1,0:T(8,128)}, f32[96,512]{1,0:T(8,128)}) async-done(((f32[96,512]{1,0:T(8,128)}, f32[96,512]{1,0:T(8,128)}), (f32[96,512]{1,0:T(8,128)}, f32[96,512]{1,0:T(8,128)})) %all-reduce.33.cloned.1.call-update) | async-done | bytes 393232 | tf_op jit(solution)/shard_map/psum | solution.py:179
  (177 shorter events, 39.0 us)
Async XLA Ops:
  6.5 12.0 %copy-start = (bf16[2,12,3,2048]{3,0,2,1:T(2,128)(2,1)S(1)}, bf16[2,12,3,2048]{3,0,2,1:T(2,128)(2,1)}, u32[]{:S(2)}) copy-start(bf16[2,12,3,2048]{3,0,2,1:T(2,128)(2,1)} %param.26) | copy-start | bytes 884740
  10.1 22.7 %all-to-all-start.2 = ((bf16[2,16,3,256]{3,0,2,1:T(2,128)(2,1)}), bf16[2,16,3,256]{3,0,2,1:T(2,128)(2,1)S(1)}, u32[]{:S(2)}, u32[]{:S(2)}) async-start(bf16[2,16,3,256]{3,0,2,1:T(2,128)(2,1)} %fusion.107), calls=%async_computation.2 | async-start | bytes 98304 | tf_op jit(solution)/shard_map/all_to_all | solution.py:109
  32.8 20.9 %all-to-all-start.1 = ((bf16[2,16,3,2048]{3,0,2,1:T(2,128)(2,1)}), bf16[2,16,3,2048]{3,0,2,1:T(2,128)(2,1)S(1)}, u32[]{:S(2)}, u32[]{:S(2)}) async-start(bf16[2,16,3,2048]{3,0,2,1:T(2,128)(2,1)} %fusion.64), calls=%async_computation.1 | async-start | bytes 786432 | tf_op jit(solution)/shard_map/all_to_all | solution.py:102
  53.8 6.9 copy-start.5
  53.8 272.5 %copy-start.15 = (f32[2,512]{1,0:T(2,128)S(1)}, f32[2,512]{1,0:T(2,128)}, u32[]{:S(2)}) copy-start(f32[2,512]{1,0:T(2,128)} %param.30) | copy-start | bytes 12292
  53.8 272.5 %copy-start.10 = (bf16[2,512,256]{2,1,0:T(8,128)(2,1)S(1)}, bf16[2,512,256]{2,1,0:T(8,128)(2,1)}, u32[]{:S(2)}) copy-start(bf16[2,512,256]{2,1,0:T(8,128)(2,1)} %param.33) | copy-start | bytes 1572868
  53.8 390.5 %all-to-all-start = ((bf16[2,16,16,128,128]{4,3,2,0,1:T(8,128)(2,1)}), bf16[2,16,16,128,128]{4,3,2,0,1:T(8,128)(2,1)}, u32[]{:S(2)}, u32[]{:S(2)}) async-start(bf16[2,16,16,128,128]{4,3,2,0,1:T(8,128)(2,1)} %select_bitcast_fusion), calls=%async_computation | async-start | bytes 33554432 | tf_op jit(solution)/shard_map/all_to_all | solution.py:95
  60.6 379.4 %all-reduce.31.cloned.1.call-start = ((), (), s32[]{:S(2)}) async-start(), calls=%async_computation.4 | async-start | bytes 6684672
  326.3 7.8 copy-start.3
  334.0 3.0 copy-start.16
  334.0 3.0 copy-start.17
  334.0 3.0 copy-start.18
  334.0 3.0 copy-start.14
  334.1 3.0 copy-start.12
  335.5 2.1 copy-start.20
  335.5 62.0 %copy-start.13 = (f32[2,2048]{1,0:T(2,128)S(1)}, f32[2,2048]{1,0:T(2,128)}, u32[]{:S(2)}) copy-start(f32[2,2048]{1,0:T(2,128)} %param.40) | copy-start | bytes 49156
  335.5 62.1 %copy-start.11 = (f32[2,4,2048]{2,1,0:T(4,128)S(1)}, f32[2,4,2048]{2,1,0:T(4,128)}, u32[]{:S(2)}) copy-start(f32[2,4,2048]{2,1,0:T(4,128)} %param.35) | copy-start | bytes 196612
  336.9 272.0 %all-reduce.35.cloned.1.call-start = ((), (), s32[]{:S(2)}) async-start(), calls=%async_computation.6 | async-start | bytes 786432 | tf_op jit(solution)/shard_map/psum | solution.py:179
  472.2 12.5 %copy-start.7 = (bf16[6,16,128,128]{3,2,1,0:T(8,128)(2,1)S(1)}, bf16[6,16,128,128]{3,2,1,0:T(8,128)(2,1)}, u32[]{:S(2)}) copy-start(bf16[6,16,128,128]{3,2,1,0:T(8,128)(2,1)} %gather_fusion.3) | copy-start | bytes 9437188
  541.0 215.1 %all-reduce.29.cloned.1.call-start = ((), (), s32[]{:S(2)}) async-start(), calls=%async_computation.3 | async-start | bytes 6684672
  643.6 7.5 copy-start.2
  644.9 7.6 copy-start.4
  655.5 241.5 %all-reduce.33.cloned.1.call-start = ((), (), s32[]{:S(2)}) async-start(), calls=%async_computation.5 | async-start | bytes 786432 | tf_op jit(solution)/shard_map/psum | solution.py:179
  760.4 12.6 %copy-start.6 = (bf16[6,16,128,128]{3,2,1,0:T(8,128)(2,1)S(1)}, bf16[6,16,128,128]{3,2,1,0:T(8,128)(2,1)}, u32[]{:S(2)}) copy-start(bf16[6,16,128,128]{3,2,1,0:T(8,128)(2,1)} %gather_fusion.6) | copy-start | bytes 9437188
  806.2 90.8 %copy-start.8 = (f32[96,512]{1,0:T(8,128)S(1)}, f32[96,512]{1,0:T(8,128)}, u32[]{:S(2)}) copy-start(f32[96,512]{1,0:T(8,128)} %get-tuple-element.42) | copy-start | bytes 589828
  806.2 90.8 %copy-start.9 = (f32[96,512]{1,0:T(8,128)S(1)}, f32[96,512]{1,0:T(8,128)}, u32[]{:S(2)}) copy-start(f32[96,512]{1,0:T(8,128)} %get-tuple-element.43) | copy-start | bytes 589828
  806.2 92.6 %copy-start.1 = (bf16[2,12,3,2048]{3,0,2,1:T(2,128)(2,1)S(1)}, bf16[2,12,3,2048]{3,0,2,1:T(2,128)(2,1)}, u32[]{:S(2)}) copy-start(bf16[2,12,3,2048]{3,0,2,1:T(2,128)(2,1)} %param.26) | copy-start | bytes 884740
  898.1 0.7 copy-start.19
Sparse Core Ops, SparseCore 0:
  337.1 102.8 all-reduce.30
  541.1 67.8 all-reduce.34
  655.7 100.3 all-reduce.28
  829.1 67.8 all-reduce.32
where the time goes:
time: 915 us; the launch traced here: 906 us
  blocking collectives  486 us (53%)
  waiting for transfers between devices  210 us (23%)
  matrix products  83.4 us (9%)
  local copies, waits for them, and re-layouts  58.1 us (6%)
  other arithmetic  30.9 us (3%)
  starting transfers between devices  22.1 us (2%)
  between operations  15 us (2%)
    psum x2, blocking collectives, on_device(): squares = lax.psum(jnp.sum(stream * stream, axis=1), 'req')  299 us
    psum x2, waiting for transfers between devices, on_device(): streams[step_idx] = stream + lax.psum(partial_out, 'head')  136 us
    unnamed x2, blocking collectives  117 us
    unnamed x6, waiting for transfers between devices  74.4 us
    all_gather x4, blocking collectives, on_device(): lax.all_gather(normed_out, 'req', axis=0, tiled=True)  70.4 us
    dot_general x4, matrix products, ssm_rows(): jnp.einsum('rhpn,rhn->rhp', new_states, c_head, precision=lax.Precision.H...  50.5 us
    squeeze x1, local copies, waits for them, and re-layouts, on_device(): arrived[0][layer_idx]  21.9 us
  transfers between devices with their start and end apart: 7, of which 4 were waited for; matrix products, arithmetic and copies ran while one was open for 6% of the time, Pallas kernels for 0%

commit v1 on v0

v1 whole, which is shorter than its diff:
```python
import jax
import jax.numpy as jnp
from jax import lax
from jax.experimental import pallas as pl
from jax.experimental.pallas import tpu as pltpu
from jax.sharding import PartitionSpec as P

MESH = pl.DeviceIdType.MESH
F32 = jnp.float32
BF16 = jnp.bfloat16
EPS = 1e-05

L = 2
D = 8192
ROWS = 192
WIDTH = 512
CH = 2048
HALF = 2304
SUB = 1152
CAP = 12


def iota(shape, dim):
    return lax.broadcasted_iota(jnp.int32, shape, dim)


def div6(v):
    return (v * 43691) >> 18


def div12(v):
    return (v * 43691) >> 19


def div24(v):
    return (v * 43691) >> 20


def div48(v):
    return (v * 43691) >> 21


def hot(cond):
    return jnp.where(cond, 1.0, 0.0).astype(BF16)


def dot(a, b):
    return jnp.dot(a, b, preferred_element_type=F32)


def silu(v):
    return v / (1.0 + jnp.exp(-v))


def softplus(v):
    return jnp.maximum(v, 0.0) + jnp.log(1.0 + jnp.exp(-jnp.abs(v)))


def body(
    emb,
    states,
    tail_x,
    tail_bc,
    pslot,
    dslot,
    norm_gain,
    w_gate,
    w_input,
    w_groups,
    w_step,
    conv_in,
    conv_grp,
    bias,
    rate,
    skip,
    out_gain,
    w_output,
    out,
    wg,
    wi,
    wb,
    ws,
    wo,
    st,
    stream,
    perm_b,
    sel_a,
    sel_b,
    pick_a,
    pick_b,
    back,
    s1s,
    s1r,
    s2s,
    s2r,
    s3s,
    s3r,
    gat,
    acc,
    hs,
    hr,
    fin,
    load_sem,
    send_sem,
    recv_sem,
    hsend_sem,
    hrecv_sem,
):
    req = lax.axis_index("req")
    head = lax.axis_index("head")
    z = req // 4
    x = req % 4
    mine = (z, x)

    def peer(axis, k):
        if axis == 0:
            return ((z + k) % 4) * 4 + x
        return z * 4 + (x + k) % 4

    loads = []
    for l in range(L):
        row = [
            (w_gate.at[l], wg.at[l]),
            (w_step.at[l], ws.at[l]),
            (w_input.at[l], wi.at[l]),
            (w_groups.at[l], wb.at[l]),
            (states.at[l], st.at[l]),
            (w_output.at[l], wo.at[l]),
        ]
        loads.append([pltpu.make_async_copy(a, b, load_sem.at[l, i]) for i, (a, b) in enumerate(row)])
        for c in loads[l]:
            c.start()

    barrier = pltpu.get_barrier_semaphore()
    for k in (1, 2, 3):
        for axis in (0, 1):
            pl.semaphore_signal(barrier, inc=1, device_id=(peer(axis, k), head), device_id_type=MESH)
    for k in range(1, 8):
        pl.semaphore_signal(barrier, inc=1, device_id=(req, (head + k) % 8), device_id_type=MESH)

    e0 = emb[0].astype(F32)
    e1 = emb[1].astype(F32)
    for g in range(4):
        stream[48 * g : 48 * g + 24, :] = e0[24 * g : 24 * g + 24]
        stream[48 * g + 24 : 48 * g + 48, :] = e1[24 * g : 24 * g + 24]

    prow = pslot[...]
    drow = dslot[...]
    diag = iota((96, 96), 0) == iota((96, 96), 1)
    pcol = jnp.sum(jnp.where(diag, prow, 0), axis=1, keepdims=True)
    dcol = jnp.sum(jnp.where(diag, drow, 0), axis=1, keepdims=True)

    n = iota((1, ROWS), 1)
    g = div48(n)
    w = n - 48 * g
    s = div24(w)
    j = w - 24 * s
    jx = div6(j)
    perm_b[...] = hot(iota((ROWS, ROWS), 0) == 48 * jx + 24 * s + 6 * g + (j - 6 * jx))

    k = iota((1, 48), 1)
    ks = div24(k)
    kj = k - 24 * ks
    kg = div6(kj)
    p = iota((128, 1), 0)
    for half in (0, 1):
        r = 24 * z + kj if half == 0 else 24 * kg + 6 * x + (kj - 6 * kg)
        slot = jnp.sum(jnp.where(dcol == r, pcol, 0), axis=0, keepdims=True)
        q = div12(slot)
        first, second = p >> 5, (p >> 3) & 3
        pq = 4 * second + first if half == 0 else 4 * first + second
        key = (pq * 4 + ((p >> 1) & 3)) * 2 + (p & 1)
        (sel_a if half == 0 else sel_b)[...] = hot(key == (q * 4 + kg) * 2 + ks)

    def tables():
        t = iota((32, 1), 0)
        c = t & 15
        owner = jnp.sum(jnp.where(prow == CAP * req + c, div6(drow) + 1, 0), axis=1, keepdims=True) - 1
        owner = jnp.where(c < CAP, owner, -1)
        u = iota((1, 64), 1)
        src, ch, other, us = u >> 4, (u >> 3) & 1, (u >> 1) & 3, u & 1
        mine_key = jnp.where(owner >= 0, owner * 2 + (t >> 4), -1)
        for half in (0, 1):
            key = (4 * src + other if half == 0 else 4 * other + src) * 2 + us
            for cs in (0, 1):
                (pick_a if half == 0 else pick_b)[cs] = hot(mine_key == jnp.where(ch == cs, key, -2))
        m = iota((ROWS, 1), 0)
        mg = div48(m)
        mw = m - 48 * mg
        ms = div24(mw)
        r = 24 * mg + mw - 24 * ms
        slot = jnp.sum(jnp.where(drow == r, prow, 0), axis=1, keepdims=True)
        want = slot * 2 + ms
        v = iota((1, 768), 1)
        blk = div48(v)
        vw = v - 48 * blk
        vsub = div24(vw)
        vv = vw - 24 * vsub
        vs = div12(vv)
        vc = vv - 12 * vs
        for half in (0, 1):
            q = (blk & 3) * 4 + (blk >> 2) if half == 0 else blk
            key = (CAP * q + vc) * 2 + vs
            for sub in (0, 1):
                back[half, sub] = hot(want == jnp.where(vsub == sub, key, -1))

    wr = iota((48, 1), 0)
    wsub = div24(wr)
    wv = wr - 24 * wsub
    wst = div12(wv)
    compact = hot(iota((48, 64), 1) == 32 * wsub + 16 * wst + (wv - 12 * wst))

    place = hot(iota((16, 256), 0) == iota((16, 256), 1))

    pl.semaphore_wait(barrier, 13)

    pending = []

    def copy(src, dst, ss, rs, dev):
        return pltpu.make_async_remote_copy(
            src_ref=src, dst_ref=dst, send_sem=ss, recv_sem=rs, device_id=dev, device_id_type=MESH
        )

    def exchange(l, phase, half, send, recv):
        axis = (phase + half) % 2
        me = mine[axis]
        e = 2 * phase + half
        got = []
        for k in (2, 1, 3):
            c = copy(
                send.at[(me + k) % 4], recv.at[me],
                send_sem.at[l, e, k], recv_sem.at[l, e, k], (peer(axis, k), head),
            )
            c.start()
            pending.append(c)
            src = (me - k) % 4
            got.append((src, copy(
                send.at[src], recv.at[src],
                send_sem.at[l, e, k], recv_sem.at[l, e, k], (peer(axis, k), head),
            )))
        return got

    for l in range(L):
        gate_load, step_load, input_load, group_load, state_load, out_load = loads[l]
        x_now = stream[...]
        lhs_a = (x_now * norm_gain[l : l + 1, :]).astype(BF16)
        squares = jnp.sum(x_now * x_now, axis=1, keepdims=True)
        gate_load.wait()
        step_load.wait()

        def project(half, lhs, weight, count, base):
            def tile(i, _):
                cols = pl.ds(pl.multiple_of(i * 256, 256), 256)
                got = dot(lhs, weight[l, :, cols])
                for g in range(4):
                    s1s[l, half, g, :, cols] = got[48 * g : 48 * g + 48].astype(BF16)
                return 0
            lax.fori_loop(0, count, tile, 0)

        project(0, lhs_a, wg, 8, 0)
        small = dot(dot(lhs_a, ws[l]).astype(BF16), place)
        small = jnp.where(iota((ROWS, 256), 1) == 16, squares, small)
        for g in range(4):
            s1s[l, 0, g, :, CH:HALF] = small[48 * g : 48 * g + 48].astype(BF16)
        got_a = exchange(l, 0, 0, s1s.at[l, 0], s1r.at[l, 0])
        lhs_b = dot(perm_b[...], lhs_a).astype(BF16)
        input_load.wait()
        group_load.wait()
        project(1, lhs_b, wi, 8, 0)
        bc = dot(lhs_b, wb[l])
        for g in range(4):
            s1s[l, 1, g, :, CH:HALF] = bc[48 * g : 48 * g + 48].astype(BF16)
        got_b = exchange(l, 0, 1, s1s.at[l, 1], s1r.at[l, 1])
        if l == 0:
            tables()

        got2 = []
        for half, got in ((0, got_a), (1, got_b)):
            for _, c in got:
                c.wait_recv()
            sel = (sel_a if half == 0 else sel_b)[...]
            me = mine[half]
            for i in range(3):
                cols = slice(768 * i, 768 * i + 768)
                total = s1s[l, half, me, :, cols].astype(F32)
                for src, _ in got:
                    total += s1r[l, half, src, :, cols].astype(F32)
                put = dot(sel, total.astype(BF16)).astype(BF16)
                for g in range(4):
                    s2s[l, half, g, :, cols] = put[32 * g : 32 * g + 32]
            got2.append(exchange(l, 1, half, s2s.at[l, half], s2r.at[l, half]))

        got3 = []
        for half in (0, 1):
            for _, c in got2[half]:
                c.wait_recv()
            me = mine[1 - half]
            for i in range(3):
                lo = slice(384 * i, 384 * i + 384)
                hi = slice(SUB + 384 * i, SUB + 384 * i + 384)
                parts = []
                for cols in (lo, hi):
                    total = s2s[l, half, me, :, cols].astype(F32)
                    for src, _ in got2[half]:
                        total += s2r[l, half, src, :, cols].astype(F32)
                    parts.append(total)
                for g in range(4):
                    rows = slice(8 * g, 8 * g + 8)
                    both = jnp.concatenate([parts[0][rows], parts[1][rows]], axis=0)
                    s3s[l, half, g, :, lo] = both.astype(BF16)
            got3.append(exchange(l, 2, half, s3s.at[l, half], s3r.at[l, half]))

        landed = []
        for half in (0, 1):
            me = mine[half]
            for _, c in got3[half]:
                c.wait_recv()
            s3r[l, half, me] = s3s[l, half, me]
            block = s3r[l, half].reshape(64, SUB)
            pick = pick_a if half == 0 else pick_b
            landed.append([dot(pick[cs], block) for cs in (0, 1)])
        (ga, gb), (xa, xb) = landed
        small = gb[:, SUB - 256 :]
        scale = lax.rsqrt(small[:, 16:17] * (1.0 / D) + EPS)
        gate_pre = jnp.concatenate([ga, gb[:, : SUB - 256]], axis=1) * scale
        x_pre = jnp.concatenate([xa, xb[:, : SUB - 256]], axis=1) * scale
        bc_pre = xb[:, SUB - 256 :] * scale
        dt_pre = small[:, :16] * scale

        def conv(pre, tails, taps):
            t0, t1, t2 = (tails[l, i].astype(F32) for i in range(3))
            c0, c1, c2, c3 = (taps[l, i : i + 1, :] for i in range(4))
            p0, p1 = pre[:16], pre[16:]
            first = t0 * c0 + t1 * c1 + t2 * c2 + p0 * c3
            second = t1 * c0 + t2 * c1 + p0.astype(BF16).astype(F32) * c2 + p1 * c3
            return silu(first), silu(second)

        bc0, bc1 = conv(bc_pre, tail_bc, conv_grp)
        b0, c0 = bc0[:, :128], bc0[:, 128:]
        b1, c1 = bc1[:, :128], bc1[:, 128:]
        both_c = jnp.concatenate([c0, c1], axis=0).astype(BF16)
        slot_of = iota((32, 1), 0) & 15
        state_load.wait()
        acc[0:32, :] = jnp.zeros((32, CH), F32)

        def contract(c, _):
            lhs = jnp.where(slot_of == c, both_c, jnp.zeros((), BF16))
            acc[0:32, :] += lax.dot_general(
                lhs, st[l, c], (((1,), (1,)), ((), ())), preferred_element_type=F32
            )
            return 0

        lax.fori_loop(0, CAP, contract, 0)

        x0, x1 = conv(x_pre, tail_x, conv_in)
        delta = softplus(dt_pre + bias[l : l + 1, :])
        decay = jnp.exp(-delta * rate[l : l + 1, :])
        direct = skip[l : l + 1, :]
        dl0, dl1 = delta[:16], delta[16:]
        de0, de1 = decay[:16], decay[16:]
        k00 = dl0 * jnp.sum(b0 * c0, axis=1, keepdims=True) + direct
        k10 = de1 * dl0 * jnp.sum(b0 * c1, axis=1, keepdims=True)
        k11 = dl1 * jnp.sum(b1 * c1, axis=1, keepdims=True) + direct
        m1 = de1 * de0
        outs = []
        for h in range(16):
            cols = slice(128 * h, 128 * h + 128)
            one = slice(h, h + 1)
            y0 = de0[:, one] * acc[0:16, cols] + k00[:, one] * x0[:, cols]
            y1 = m1[:, one] * acc[16:32, cols] + k10[:, one] * x0[:, cols] + k11[:, one] * x1[:, cols]
            outs.append(jnp.concatenate([y0, y1], axis=0))
        gated = jnp.concatenate(outs, axis=1) * silu(gate_pre)
        mean_sq = jnp.sum(gated * gated, axis=1, keepdims=True) * (1.0 / CH)
        normed = (gated * lax.rsqrt(mean_sq + EPS) * out_gain[l : l + 1, :]).astype(BF16)

        for half in (0, 1):
            a, b = mine[1 - half], mine[half]
            cols = 1024 * half
            stacked = jnp.concatenate([normed[:, cols : cols + 512], normed[:, cols + 512 : cols + 1024]], axis=0)
            gat[l, half, a, b] = dot(compact, stacked).astype(BF16)
        gots = []
        for half in (0, 1):
            axis = half
            a, b = mine[1 - half], mine[half]
            e = 6 + half
            got = []
            for k in (2, 1, 3):
                sems = (send_sem.at[l, e, k], recv_sem.at[l, e, k], (peer(axis, k), head))
                c = copy(gat.at[l, half, a, b], gat.at[l, half, a, b], *sems)
                c.start()
                pending.append(c)
                src = (b - k) % 4
                got.append(copy(gat.at[l, half, a, src], gat.at[l, half, a, src], *sems))
            gots.append(got)
        lasts = []
        for half in (0, 1):
            axis = 1 - half
            a = mine[1 - half]
            e = 8 + half
            for c in gots[half]:
                c.wait_recv()
            got = []
            for k in (2, 1, 3):
                sems = (send_sem.at[l, e, k], recv_sem.at[l, e, k], (peer(axis, k), head))
                c = copy(gat.at[l, half, a], gat.at[l, half, a], *sems)
                c.start()
                pending.append(c)
                src = (a - k) % 4
                got.append(copy(gat.at[l, half, src], gat.at[l, half, src], *sems))
            lasts.append(got)
        out_load.wait()
        acc_now = acc.at[0:ROWS, 0:WIDTH]
        for half in (0, 1):
            for c in lasts[half]:
                c.wait_recv()
            rows = gat[l, half].reshape(768, 512)
            for sub in (0, 1):
                lhs = dot(back[half, sub], rows).astype(BF16)
                base = 1024 * half + 512 * sub
                part = dot(lhs, wo[l, base : base + 512, :])
                if half + sub == 0:
                    acc_now[...] = part
                else:
                    acc_now[...] += part

        for h in range(8):
            i, c = h // 4, h % 4
            hs[l, h] = acc[96 * i : 96 * i + 96, 128 * c : 128 * c + 128].astype(BF16)
        got = []
        for k in (4, 3, 5, 2, 6, 1, 7):
            dev = (req, (head + k) % 8)
            sems = (hsend_sem.at[l, 0, k], hrecv_sem.at[l, 0, k], dev)
            c = copy(hs.at[l, (head + k) % 8], hr.at[l, head], *sems)
            c.start()
            pending.append(c)
            src = (head - k) % 8
            got.append((src, copy(hs.at[l, src], hr.at[l, src], *sems)))
        total = hs[l, head].astype(F32)
        for src, c in got:
            c.wait_recv()
            total += hr[l, src].astype(F32)
        fin[l, head] = total.astype(BF16)
        got = []
        for k in (4, 3, 5, 2, 6, 1, 7):
            dev = (req, (head + k) % 8)
            sems = (hsend_sem.at[l, 1, k], hrecv_sem.at[l, 1, k], dev)
            c = copy(fin.at[l, head], fin.at[l, head], *sems)
            c.start()
            pending.append(c)
            src = (head - k) % 8
            got.append(copy(fin.at[l, src], fin.at[l, src], *sems))
        for c in got:
            c.wait_recv()
        for h in range(8):
            i, c = h // 4, h % 4
            stream[96 * i : 96 * i + 96, 128 * c : 128 * c + 128] += fin[l, h].astype(F32)

    whole = stream[...]
    for s in (0, 1):
        parts = [whole[48 * g + 24 * s : 48 * g + 24 * s + 24] for g in range(4)]
        out[s] = jnp.concatenate(parts, axis=0).astype(BF16)
    for c in pending:
        c.wait_send()


def on_device(
    embedded,
    ssm_states,
    conv_tail_x,
    conv_tail_bc,
    prefill_slot,
    decode_slot,
    norm_gain,
    w_gate,
    w_input,
    w_groups,
    w_step,
    conv_input,
    conv_groups,
    step_bias,
    decay_rate,
    skip_gain,
    out_gain,
    w_output,
):
    vmem = pl.BlockSpec(memory_space=pltpu.VMEM)
    hbm = pl.BlockSpec(memory_space=pl.ANY)

    def by_tap(tails):
        return jnp.pad(jnp.swapaxes(tails, 1, 2), ((0, 0), (0, 0), (0, 4), (0, 0)))

    return pl.pallas_call(
        body,
        out_shape=jax.ShapeDtypeStruct((2, 96, WIDTH), BF16),
        in_specs=[vmem, hbm, vmem, vmem, vmem, vmem, vmem, hbm, hbm, hbm, hbm, vmem, vmem, vmem, vmem, vmem, vmem, hbm],
        out_specs=vmem,
        scratch_shapes=[
            pltpu.VMEM((L, WIDTH, CH), BF16),
            pltpu.VMEM((L, WIDTH, CH), BF16),
            pltpu.VMEM((L, WIDTH, 256), BF16),
            pltpu.VMEM((L, WIDTH, 16), BF16),
            pltpu.VMEM((L, CH, WIDTH), BF16),
            pltpu.VMEM((L, CAP, CH, 128), BF16),
            pltpu.VMEM((ROWS, WIDTH), F32),
            pltpu.VMEM((ROWS, ROWS), BF16),
            pltpu.VMEM((128, 48), BF16),
            pltpu.VMEM((128, 48), BF16),
            pltpu.VMEM((2, 32, 64), BF16),
            pltpu.VMEM((2, 32, 64), BF16),
            pltpu.VMEM((2, 2, ROWS, 768), BF16),
            pltpu.VMEM((L, 2, 4, 48, HALF), BF16),
            pltpu.VMEM((L, 2, 4, 48, HALF), BF16),
            pltpu.VMEM((L, 2, 4, 32, HALF), BF16),
            pltpu.VMEM((L, 2, 4, 32, HALF), BF16),
            pltpu.VMEM((L, 2, 4, 16, SUB), BF16),
            pltpu.VMEM((L, 2, 4, 16, SUB), BF16),
            pltpu.VMEM((L, 2, 4, 4, 48, 512), BF16),
            pltpu.VMEM((ROWS, CH), F32),
            pltpu.VMEM((L, 8, 96, 128), BF16),
            pltpu.VMEM((L, 8, 96, 128), BF16),
            pltpu.VMEM((L, 8, 96, 128), BF16),
            pltpu.SemaphoreType.DMA((L, 6)),
            pltpu.SemaphoreType.DMA((L, 10, 4)),
            pltpu.SemaphoreType.DMA((L, 10, 4)),
            pltpu.SemaphoreType.DMA((L, 2, 8)),
            pltpu.SemaphoreType.DMA((L, 2, 8)),
        ],
        compiler_params=pltpu.CompilerParams(
            collective_id=0, has_side_effects=True, vmem_limit_bytes=58 * 2**20
        ),
    )(
        embedded,
        ssm_states.reshape(L, CAP, CH, 128),
        by_tap(conv_tail_x),
        by_tap(conv_tail_bc),
        prefill_slot.reshape(1, 96),
        decode_slot.reshape(1, 96),
        norm_gain,
        w_gate,
        w_input,
        w_groups,
        w_step,
        conv_input,
        conv_groups,
        step_bias,
        decay_rate,
        skip_gain,
        out_gain,
        w_output,
    )


def solution(mesh):
    return jax.shard_map(
        on_device,
        mesh=mesh,
        in_specs=(
            P(None, None, "req"),
            P(None, "req", "head", None, None),
            P(None, "req", None, "head"),
            P(None, "req", None, "head"),
            P(),
            P(),
            P(None, "req"),
            P(None, "req", "head"),
            P(None, "req", "head"),
            P(None, "req", "head"),
            P(None, "req", "head"),
            P(None, None, "head"),
            P(None, None, "head"),
            P(None, "head"),
            P(None, "head"),
            P(None, "head"),
            P(None, "head"),
            P(None, "head", "req"),
        ),
        out_specs=P(None, None, "req"),
        check_vma=False,
    )
```

time: 915 us -> 132 us (0.14)
  blocking collectives: 486 us -> 0 us
  waiting for transfers between devices: 210 us -> 0 us
  Pallas kernels: 0 us -> 125 us
  matrix products: 83.4 us -> 0 us
  local copies, waits for them, and re-layouts: 58.1 us -> 6.45 us
  other arithmetic: 30.9 us -> 0 us
  starting transfers between devices: 22.1 us -> 0 us
  between operations: 15 us -> 0.02 us
    psum x2 -> x0, blocking collectives: 299 us -> none  [on_device(): squares = lax.psum(jnp.sum(stream * stream, axis=1), 'req')]
    psum x2 -> x0, waiting for transfers between devices: 136 us -> none  [on_device(): streams[step_idx] = stream + lax.psum(partial_out, 'head')]
    pallas_call x0 -> x1, Pallas kernels: none -> 125 us  [on_device(): pl.pallas_call(body, out_shape=jax.ShapeDtypeStruct((2, 96, WIDTH), BF16)...]
    unnamed x2 -> x0, blocking collectives: 117 us -> none
    dot_general x24 -> x0, matrix products: 83.4 us -> none  [the longest x4 50.5 us: ssm_rows(): jnp.einsum('rhpn,rhn->rhp', new_states, c_head, precision=lax.Precision.H...]
    unnamed x6 -> x0, waiting for transfers between devices: 74.4 us -> none
    all_gather x4 -> x0, blocking collectives: 70.4 us -> none  [on_device(): lax.all_gather(normed_out, 'req', axis=0, tiled=True)]
    gather x9 -> x0, local copies, waits for them, and re-layouts: 29 us -> none  [the longest x3 14.5 us: pick_slots(): picked = jnp.take(block, slots, axis=axis)]
  transfers between devices with their start and end apart: 7 -> 0, of which waited for: 4 -> 0; matrix products, arithmetic and copies ran while one was open for 6% -> 0% of each run, Pallas kernels for 0% -> 0%
where the time goes in v1:
time: 132 us
  Pallas kernels  125 us (95%)
  local copies, waits for them, and re-layouts  6.45 us (5%)
    pallas_call x1, Pallas kernels, on_device(): pl.pallas_call(body, out_shape=jax.ShapeDtypeStruct((2, 96, WIDTH), BF16)...  125 us
    unnamed x4, local copies, waits for them, and re-layouts  5.04 us

profile of v1, /device:TPU:1, one launch (start us, length us, event | category | flops | bytes accessed | tf_op | source)
XLA Modules:
  0.0 131.6 jit_solution(17763218726991410699)
XLA Ops:
  0.0 1.1 copy.24
  1.1 0.8 pad.8.tail_x
  1.8 1.6 %copy.21.w_step = bf16[2,512,16]{2,1,0:T(8,128)(2,1)} copy(bf16[2,512,16]{1,2,0:T(8,128)(2,1)} %param.28) | data formatting | bytes 65536 | tf_op args[10]
  3.4 0.8 copy.25
  4.2 0.6 pad.9.tail_bc
  4.8 125.1 %shard_map.172 = bf16[2,96,512]{2,1,0:T(8,128)(2,1)} custom-call(bf16[2,96,512]{2,1,0:T(8,128)(2,1)} %emb.1, bf16[2,12,2048,128]{3,2,1,0:T(8,128)(2,1)} %bitcast.9, bf16[2,3,16,2048]{3,2,1,0:T(8,128)(2,1)} %pad.8.tail_x, bf16[2,3,16,256]{3,2,1,0:T(8,128)(2,1)} %pad.9.tail_bc, s32[1,96]{1,0:T(1,128)} %bitcast.12, s32[1,96]{1,0:T(1,128)} %bitcast.13, ...), custom_call_target="tpu_custom_call" | custom-call | tf_op jit(solution)/shard_map/pallas_call | solution.py:492
  129.9 1.6 %copy.27 = bf16[2,96,512]{2,1,0:T(8,128)(2,1)} copy(bf16[2,96,512]{2,1,0:T(8,128)(2,1)} %shard_map.172) | data formatting | bytes 393216

commit v2 on v1

v2 whole, which is shorter than its diff:
```python
import jax
import jax.numpy as jnp
from jax import lax
from jax.experimental import pallas as pl
from jax.experimental.pallas import tpu as pltpu
from jax.sharding import PartitionSpec as P

MESH = pl.DeviceIdType.MESH
F32 = jnp.float32
BF16 = jnp.bfloat16
EPS = 1e-05

L = 2
D = 8192
ROWS = 96
WIDTH = 512
CH = 2048
S = 2
PART = 1152
CAP = 12


def iota(shape, dim):
    return lax.broadcasted_iota(jnp.int32, shape, dim)


def div6(v):
    return (v * 43691) >> 18


def div12(v):
    return (v * 43691) >> 19


def div24(v):
    return (v * 43691) >> 20


def div48(v):
    return (v * 43691) >> 21


def hot(cond):
    return jnp.where(cond, 1.0, 0.0).astype(BF16)


def dot(a, b):
    return jnp.dot(a, b, preferred_element_type=F32)


def dot_t(a, b):
    return lax.dot_general(a, b, (((1,), (1,)), ((), ())), preferred_element_type=F32)


def silu(v):
    return v / (1.0 + jnp.exp(-v))


def softplus(v):
    return jnp.maximum(v, 0.0) + jnp.log(1.0 + jnp.exp(-jnp.abs(v)))


def body(
    emb_h,
    states,
    tail_x_h,
    tail_bc_h,
    pslot_h,
    dslot_h,
    norm_gain_h,
    w_gate,
    w_input,
    w_groups,
    w_step,
    conv_in_h,
    conv_grp_h,
    bias_h,
    rate_h,
    skip_h,
    out_gain_h,
    w_output,
    out,
    emb,
    tail_x2,
    tail_bc2,
    pslot,
    dslot,
    norm_gain,
    conv_in,
    conv_grp,
    bias,
    rate,
    skip,
    out_gain,
    tail_x,
    tail_bc,
    small_sem,
    wg,
    wi,
    wb,
    ws,
    wo,
    st,
    stream,
    perm_b,
    sel_a,
    sel_b,
    pick_a,
    pick_b,
    back,
    s1s,
    s1r,
    s2s,
    s2r,
    s3s,
    s3r,
    gat,
    held,
    hs,
    hr,
    fin,
    load_sem,
    send_sem,
    recv_sem,
    gsend_sem,
    grecv_sem,
    hsend_sem,
    hrecv_sem,
):
    req = lax.axis_index("req")
    head = lax.axis_index("head")
    z = req // 4
    x = req % 4
    mine = (z, x)

    def peer(axis, k):
        if axis == 0:
            return ((z + k) % 4) * 4 + x
        return z * 4 + (x + k) % 4

    loads = []
    for l in range(L):
        row = [
            (w_gate.at[l], wg.at[l]),
            (w_step.at[l], ws.at[l]),
            (w_input.at[l], wi.at[l]),
            (w_groups.at[l], wb.at[l]),
            (states.at[l], st.at[l]),
            (w_output.at[l], wo.at[l]),
        ]
        loads.append([pltpu.make_async_copy(a, b, load_sem.at[l, i]) for i, (a, b) in enumerate(row)])
    first = [(pslot_h, pslot), (dslot_h, dslot), (emb_h, emb), (norm_gain_h, norm_gain)]
    later = [
        (tail_x_h, tail_x2),
        (tail_bc_h, tail_bc2),
        (conv_in_h, conv_in),
        (conv_grp_h, conv_grp),
        (bias_h, bias),
        (rate_h, rate),
        (skip_h, skip),
        (out_gain_h, out_gain),
    ]
    first = [pltpu.make_async_copy(a, b, small_sem.at[i]) for i, (a, b) in enumerate(first)]
    later = [pltpu.make_async_copy(a, b, small_sem.at[4 + i]) for i, (a, b) in enumerate(later)]
    for c in first + loads[0] + later:
        c.start()

    barrier = pltpu.get_barrier_semaphore()
    for k in (1, 2, 3):
        for axis in (0, 1):
            pl.semaphore_signal(barrier, inc=1, device_id=(peer(axis, k), head), device_id_type=MESH)
    for k in range(1, 8):
        pl.semaphore_signal(barrier, inc=1, device_id=(req, (head + k) % 8), device_id_type=MESH)

    for c in first:
        c.wait()

    for t in range(S):
        stream[t] = emb[t].astype(F32)

    prow = pslot[...]
    drow = dslot[...]
    diag = iota((96, 96), 0) == iota((96, 96), 1)
    pcol = jnp.sum(jnp.where(diag, prow, 0), axis=1, keepdims=True)
    dcol = jnp.sum(jnp.where(diag, drow, 0), axis=1, keepdims=True)

    n = iota((1, ROWS), 1)
    g = div24(n)
    j = n - 24 * g
    jx = div6(j)
    perm_b[...] = hot(iota((ROWS, ROWS), 0) == 24 * jx + 6 * g + (j - 6 * jx))

    k = iota((1, 48), 1)
    kp = div24(k)
    kj = k - 24 * kp
    kg = div6(kj)
    p = iota((128, 1), 0)
    for half in (0, 1):
        r = 24 * z + kj if half == 0 else 24 * kg + 6 * x + (kj - 6 * kg)
        slot = jnp.sum(jnp.where(dcol == r, pcol, 0), axis=0, keepdims=True)
        q = div12(slot)
        first, second = p >> 5, (p >> 3) & 3
        pq = 4 * second + first if half == 0 else 4 * first + second
        key = (pq * 4 + (p & 3)) * 2 + ((p >> 2) & 1)
        (sel_a if half == 0 else sel_b)[...] = hot(key == (q * 4 + kg) * 2 + kp)

    def tables():
        t = iota((32, 1), 0)
        c = t & 15
        owner = jnp.sum(jnp.where(prow == CAP * req + c, div6(drow) + 1, 0), axis=1, keepdims=True) - 1
        mine_key = jnp.where((owner >= 0) & (c < CAP), owner * 2 + (t >> 4), -1)
        u = iota((1, 32), 1)
        src, up, other = u >> 3, (u >> 2) & 1, u & 3
        for half in (0, 1):
            key = (4 * src + other if half == 0 else 4 * other + src) * 2 + up
            (pick_a if half == 0 else pick_b)[...] = hot(mine_key == key)
        want = jnp.sum(jnp.where(drow == iota((ROWS, 1), 0), prow, 0), axis=1, keepdims=True)
        v = iota((1, 768), 1)
        blk = div48(v)
        vw = v - 48 * blk
        vsub = div12(vw)
        vc = vw - 12 * vsub
        for half in (0, 1):
            q = (blk & 3) * 4 + (blk >> 2) if half == 0 else blk
            for sub in range(4):
                back[half, sub] = hot(want == jnp.where(vsub == sub, CAP * q + vc, -1))

    wr = iota((48, 1), 0)
    wsub = div12(wr)
    compact = hot(iota((48, 64), 1) == 16 * wsub + (wr - 12 * wsub))

    place = hot(iota((16, 128), 0) == iota((16, 128), 1))

    pl.semaphore_wait(barrier, 13)

    def drain(l, t, phase):
        for half in (0, 1):
            f = flights.pop((l, t, phase, half), None)
            if f is not None:
                f.wait_send()

    def copy(src, dst, ss, rs, dev):
        return pltpu.make_async_remote_copy(
            src_ref=src, dst_ref=dst, send_sem=ss, recv_sem=rs, device_id=dev, device_id_type=MESH
        )

    flights = {}
    others = {}

    def exchange(l, t, phase, half):
        send, recv = ((s1s, s1r), (s2s, s2r), (s3s, s3r))[phase]
        axis = (phase + half) % 2
        me = mine[axis]
        e = 2 * phase + half
        sems = (send_sem.at[t, e], recv_sem.at[t, e])
        for k in (2, 1, 3):
            copy(send.at[l, t, half, (me + k) % 4], recv.at[l, t, half, me], *sems, (peer(axis, k), head)).start()
        three = (send.at[l, t, half, 0:3], recv.at[l, t, half, 0:3])
        flights[l, t, phase, half] = copy(*three, *sems, (peer(axis, 1), head))
        others[l, t, phase, half] = [(me + k) % 4 for k in (1, 2, 3)]

    waited = set()

    def ready(l, i):
        if (l, i) not in waited:
            waited.add((l, i))
            loads[l][i].wait()

    def project(l, steps):
        many = len(steps)
        x_now = jnp.concatenate([stream[t] for t in steps], axis=0)
        lhs_a = (x_now * norm_gain[l : l + 1, :]).astype(BF16)
        lhs_b = jnp.concatenate(
            [dot(perm_b[...], lhs_a[ROWS * i : ROWS * i + ROWS]).astype(BF16) for i in range(many)], axis=0
        )
        squares = jnp.sum(x_now * x_now, axis=1, keepdims=True)

        def put(half, cols, low, high):
            for i, t in enumerate(steps):
                for g in range(4):
                    rows = slice(ROWS * i + 24 * g, ROWS * i + 24 * g + 24)
                    s1s[l, t, half, g, :, cols] = jnp.concatenate([low[rows], high[rows]], axis=0).astype(BF16)

        def main(half, lhs, weight):
            def tile(i, _):
                at = pl.multiple_of(i * 256, 256)
                low = dot(lhs, weight[l, :, pl.ds(at, 256)])
                high = dot(lhs, weight[l, :, pl.ds(pl.multiple_of(at + 1024, 256), 256)])
                put(half, pl.ds(at, 256), low, high)
                return 0

            lax.fori_loop(0, 4, tile, 0)

        end = slice(1024, PART)
        ready(l, 1)
        small = dot(dot_t(lhs_a, ws[l]).astype(BF16), place)
        small = jnp.where(iota((ROWS * many, 128), 1) == 16, squares, small)
        put(0, end, small, jnp.zeros_like(small))
        ready(l, 0)
        main(0, lhs_a, wg)
        for t in steps:
            exchange(l, t, 0, 0)
        ready(l, 3)
        bc = dot(lhs_b, wb[l])
        put(1, end, bc[:, :128], bc[:, 128:])
        ready(l, 2)
        main(1, lhs_b, wi)
        for t in steps:
            exchange(l, t, 0, 1)

    def second(l, t):
        for half in (0, 1):
            flights[l, t, 0, half].wait_recv()
            total = s1s[l, t, half, mine[half]].astype(F32)
            for src in others[l, t, 0, half]:
                total += s1r[l, t, half, src].astype(F32)
            put = dot((sel_a if half == 0 else sel_b)[...], total.astype(BF16)).astype(BF16)
            for g in range(4):
                s2s[l, t, half, g] = put[32 * g : 32 * g + 32]
            exchange(l, t, 1, half)

    def third(l, t):
        for half in (0, 1):
            flights[l, t, 1, half].wait_recv()
            total = s2s[l, t, half, mine[1 - half]].astype(F32)
            for src in others[l, t, 1, half]:
                total += s2r[l, t, half, src].astype(F32)
            for g in range(4):
                s3s[l, t, half, g] = total[8 * g : 8 * g + 8]
            exchange(l, t, 2, half)

    def landed(l, t, half):
        me = mine[half]
        flights[l, t, 2, half].wait_recv()
        s3r[l, t, half, me] = s3s[l, t, half, me]
        block = s3r[l, t, half].reshape(32, PART)
        pick = (pick_a if half == 0 else pick_b)[...]
        high = block.astype(BF16)
        low = (block - high.astype(F32)).astype(BF16)
        both = dot(pick, high) + dot(pick, low)
        main = jnp.concatenate([both[:16, :1024], both[16:, :1024]], axis=1)
        return main, both[:16, 1024:], both[16:, 1024:]

    kept = {}

    def conv(l, pre, old, tails, taps):
        tap = [taps[l, i : i + 1, :] for i in range(4)]
        tail = [tails[48 * l + 16 * i : 48 * l + 16 * i + 16, :] for i in range(3)]
        seq = (tail + [pre]) if old is None else (tail[1:] + [old.astype(BF16).astype(F32), pre])
        return silu(seq[0] * tap[0] + seq[1] * tap[1] + seq[2] * tap[2] + seq[3] * tap[3])

    def scan(l, t):
        xm, xb, xc = landed(l, t, 1)
        gm, small, _ = landed(l, t, 0)
        scale = lax.rsqrt(small[:, 16:17] * (1.0 / D) + EPS)
        dt_pre = small[:, :16] * scale
        bc_pre = jnp.concatenate([xb, xc], axis=1) * scale
        x_pre = xm * scale
        old = kept.get(l)
        bc = conv(l, bc_pre, old and old[0], tail_bc, conv_grp)
        b_now, c_now = bc[:, :128], bc[:, 128:]
        c_low = c_now.astype(BF16)
        slot_of = iota((16, 1), 0)
        ready(l, 4)
        held[...] = jnp.zeros_like(held)

        zero = jnp.zeros((), BF16)

        def contract(i, _):
            c = 2 * i
            lhs = jnp.concatenate([jnp.where(slot_of == c, c_low, zero), jnp.where(slot_of == c + 1, c_low, zero)], axis=1)
            for j in range(4):
                rows = slice(512 * j, 512 * j + 512)
                pair = jnp.concatenate([st[l, c, rows, :], st[l, c + 1, rows, :]], axis=1)
                held[:, rows] += dot_t(lhs, pair)
            return 0

        lax.fori_loop(0, CAP // 2, contract, 0)
        delta = softplus(dt_pre + bias[l : l + 1, :])
        decay = jnp.exp(-delta * rate[l : l + 1, :])
        x_now = conv(l, x_pre, old and old[1], tail_x, conv_in)
        k_now = delta * jnp.sum(b_now * c_now, axis=1, keepdims=True) + skip[l : l + 1, :]
        if t == 0:
            kept[l] = (bc_pre, x_pre, b_now, x_now, delta, decay)
            k_state = decay
        else:
            _, _, b_old, x_old, delta_old, decay_old = old
            k_state = decay * decay_old
            k_old = decay * delta_old * jnp.sum(b_old * c_now, axis=1, keepdims=True)
        outs = []
        for h in range(16):
            cols = slice(128 * h, 128 * h + 128)
            one = slice(h, h + 1)
            y = k_state[:, one] * held[:, cols] + k_now[:, one] * x_now[:, cols]
            if t == 1:
                y += k_old[:, one] * x_old[:, cols]
            outs.append(y)
        gated = jnp.concatenate(outs, axis=1) * silu(gm * scale)
        mean_sq = jnp.sum(gated * gated, axis=1, keepdims=True) * (1.0 / CH)
        normed = (gated * lax.rsqrt(mean_sq + EPS) * out_gain[l : l + 1, :]).astype(BF16)
        for half in (0, 1):
            quarters = [normed[:, 1024 * half + 256 * i : 1024 * half + 256 * i + 256] for i in range(4)]
            gat[l, t, half, mine[1 - half], mine[half]] = dot(compact, jnp.concatenate(quarters, axis=0)).astype(BF16)
            gather(l, t, 0, half)

    def gather(l, t, stage, half):
        a, b = mine[1 - half], mine[half]
        axis = half if stage == 0 else 1 - half
        sems = (gsend_sem.at[t, stage, half], grecv_sem.at[t, stage, half])
        here = gat.at[l, t, half, a, b] if stage == 0 else gat.at[l, t, half, a]
        for k in (2, 1, 3):
            copy(here, here, *sems, (peer(axis, k), head)).start()
        three = gat.at[l, t, half, a, 0:3] if stage == 0 else gat.at[l, t, half, 0:3]
        flights[l, t, 3 + stage, half] = copy(three, three, *sems, (peer(axis, 1), head))

    def forward(l, t):
        for half in (0, 1):
            flights[l, t, 3, half].wait_recv()
            gather(l, t, 1, half)

    def to_heads(l, t, stage):
        sems = (hsend_sem.at[t, stage], hrecv_sem.at[t, stage])
        for k in (4, 3, 5, 2, 6, 1, 7):
            to = (head + k) % 8
            pair = (hs.at[l, t, to], hr.at[l, t, head]) if stage == 0 else (fin.at[l, t, head], fin.at[l, t, head])
            copy(*pair, *sems, (req, to)).start()
        seven = (hs.at[l, t, 0:7], hr.at[l, t, 0:7]) if stage == 0 else (fin.at[l, t, 0:7], fin.at[l, t, 0:7])
        flights[l, t, 5 + stage, 0] = copy(*seven, *sems, (req, (head + 1) % 8))

    def output(l, t):
        ready(l, 5)
        part = None
        for half in (0, 1):
            flights[l, t, 4, half].wait_recv()
            rows = gat[l, t, half].reshape(768, 256)
            lhs = jnp.concatenate([dot(back[half, sub], rows).astype(BF16) for sub in range(4)], axis=1)
            more = dot(lhs, wo[l, 1024 * half : 1024 * half + 1024, :])
            part = more if part is None else part + more
        for h in range(8):
            i, c = h // 4, h % 4
            hs[l, t, h] = part[48 * i : 48 * i + 48, 128 * c : 128 * c + 128].astype(BF16)
        to_heads(l, t, 0)

    def reduce(l, t):
        total = hs[l, t, head].astype(F32)
        flights[l, t, 5, 0].wait_recv()
        for k in range(1, 8):
            total += hr[l, t, (head + k) % 8].astype(F32)
        fin[l, t, head] = total.astype(BF16)
        to_heads(l, t, 1)

    def finish(l, t):
        flights[l, t, 6, 0].wait_recv()
        for h in range(8):
            i, c = h // 4, h % 4
            rows, cols = slice(48 * i, 48 * i + 48), slice(128 * c, 128 * c + 128)
            now = stream[t, rows, cols] + fin[l, t, h].astype(F32)
            if l < L - 1:
                stream[t, rows, cols] = now
            else:
                out[t, rows, cols] = now.astype(BF16)

    project(0, (0, 1))
    tables()
    for c in later:
        c.wait()
    t = iota((96, 1), 0)
    tl = div48(t)
    tk = (t - 48 * tl) >> 4
    by_layer = hot((iota((96, 72), 1) == (t & 15) * 6 + 2 * tk + tl) & ((t & 15) < CAP))
    for tails, rows in ((tail_x2, tail_x), (tail_bc2, tail_bc)):
        for i in range(36):
            rows[2 * i : 2 * i + 2, :] = tails[i].astype(F32)
        rows[...] = dot(by_layer, rows[0:72, :].astype(BF16))
    for l in range(L):
        second(l, 0)
        second(l, 1)
        if l == 0:
            for c in loads[1]:
                c.start()
        third(l, 0)
        drain(l, 0, 0)
        third(l, 1)
        drain(l, 1, 0)
        scan(l, 0)
        scan(l, 1)
        forward(l, 0)
        drain(l, 0, 1)
        drain(l, 0, 2)
        drain(l, 1, 1)
        drain(l, 1, 2)
        forward(l, 1)
        drain(l, 0, 3)
        drain(l, 1, 3)
        output(l, 0)
        output(l, 1)
        drain(l, 0, 4)
        reduce(l, 0)
        drain(l, 1, 4)
        reduce(l, 1)
        drain(l, 0, 5)
        finish(l, 0)
        if l < L - 1:
            project(l + 1, (0,))
        drain(l, 1, 5)
        finish(l, 1)
        if l < L - 1:
            project(l + 1, (1,))
        drain(l, 0, 6)
        drain(l, 1, 6)
    for key in list(flights):
        drain(*key[:3])


def on_device(
    embedded,
    ssm_states,
    conv_tail_x,
    conv_tail_bc,
    prefill_slot,
    decode_slot,
    norm_gain,
    w_gate,
    w_input,
    w_groups,
    w_step,
    conv_input,
    conv_groups,
    step_bias,
    decay_rate,
    skip_gain,
    out_gain,
    w_output,
):
    vmem = pl.BlockSpec(memory_space=pltpu.VMEM)
    hbm = pl.BlockSpec(memory_space=pl.ANY)

    def by_slot(tails):
        return jnp.transpose(tails, (1, 2, 0, 3)).reshape(CAP * 3, L, tails.shape[3])

    return pl.pallas_call(
        body,
        out_shape=jax.ShapeDtypeStruct((2, 96, WIDTH), BF16),
        in_specs=[hbm] * 18,
        out_specs=vmem,
        scratch_shapes=[
            pltpu.VMEM((2, 96, WIDTH), BF16),
            pltpu.VMEM((3 * CAP, L, CH), BF16),
            pltpu.VMEM((3 * CAP, L, 256), BF16),
            pltpu.VMEM((1, 96), jnp.int32),
            pltpu.VMEM((1, 96), jnp.int32),
            pltpu.VMEM((L, WIDTH), F32),
            pltpu.VMEM((L, 4, CH), F32),
            pltpu.VMEM((L, 4, 256), F32),
            pltpu.VMEM((L, 16), F32),
            pltpu.VMEM((L, 16), F32),
            pltpu.VMEM((L, 16), F32),
            pltpu.VMEM((L, CH), F32),
            pltpu.VMEM((96, CH), F32),
            pltpu.VMEM((96, 256), F32),
            pltpu.SemaphoreType.DMA((12,)),
            pltpu.VMEM((L, WIDTH, CH), BF16),
            pltpu.VMEM((L, WIDTH, CH), BF16),
            pltpu.VMEM((L, WIDTH, 256), BF16),
            pltpu.VMEM((L, 16, WIDTH), BF16),
            pltpu.VMEM((L, CH, WIDTH), BF16),
            pltpu.VMEM((L, CAP, CH, 128), BF16),
            pltpu.VMEM((S, ROWS, WIDTH), F32),
            pltpu.VMEM((ROWS, ROWS), BF16),
            pltpu.VMEM((128, 48), BF16),
            pltpu.VMEM((128, 48), BF16),
            pltpu.VMEM((32, 32), BF16),
            pltpu.VMEM((32, 32), BF16),
            pltpu.VMEM((2, 4, ROWS, 768), BF16),
            pltpu.VMEM((L, S, 2, 4, 48, PART), BF16),
            pltpu.VMEM((L, S, 2, 4, 48, PART), BF16),
            pltpu.VMEM((L, S, 2, 4, 32, PART), BF16),
            pltpu.VMEM((L, S, 2, 4, 32, PART), BF16),
            pltpu.VMEM((L, S, 2, 4, 8, PART), F32),
            pltpu.VMEM((L, S, 2, 4, 8, PART), F32),
            pltpu.VMEM((L, S, 2, 4, 4, 48, 256), BF16),
            pltpu.VMEM((16, CH), F32),
            pltpu.VMEM((L, S, 8, 48, 128), BF16),
            pltpu.VMEM((L, S, 8, 48, 128), BF16),
            pltpu.VMEM((L, S, 8, 48, 128), BF16),
            pltpu.SemaphoreType.DMA((L, 6)),
            pltpu.SemaphoreType.DMA((S, 6)),
            pltpu.SemaphoreType.DMA((S, 6)),
            pltpu.SemaphoreType.DMA((S, 2, 2)),
            pltpu.SemaphoreType.DMA((S, 2, 2)),
            pltpu.SemaphoreType.DMA((S, 2)),
            pltpu.SemaphoreType.DMA((S, 2)),
        ],
        compiler_params=pltpu.CompilerParams(
            collective_id=0, has_side_effects=True, vmem_limit_bytes=58 * 2**20
        ),
    )(
        embedded,
        ssm_states.reshape(L, CAP, CH, 128),
        by_slot(conv_tail_x),
        by_slot(conv_tail_bc),
        prefill_slot.reshape(1, 96),
        decode_slot.reshape(1, 96),
        norm_gain,
        w_gate,
        w_input,
        w_groups,
        jnp.swapaxes(w_step, 1, 2),
        conv_input,
        conv_groups,
        step_bias,
        decay_rate,
        skip_gain,
        out_gain,
        w_output,
    )


def solution(mesh):
    return jax.shard_map(
        on_device,
        mesh=mesh,
        in_specs=(
            P(None, None, "req"),
            P(None, "req", "head", None, None),
            P(None, "req", None, "head"),
            P(None, "req", None, "head"),
            P(),
            P(),
            P(None, "req"),
            P(None, "req", "head"),
            P(None, "req", "head"),
            P(None, "req", "head"),
            P(None, "req", "head"),
            P(None, None, "head"),
            P(None, None, "head"),
            P(None, "head"),
            P(None, "head"),
            P(None, "head"),
            P(None, "head"),
            P(None, "head", "req"),
        ),
        out_specs=P(None, None, "req"),
        check_vma=False,
    )
```

time: 132 us -> 106 us (0.80)
  Pallas kernels: 125 us -> 104 us
  local copies, waits for them, and re-layouts: 6.45 us -> 1.62 us
    pallas_call x1, Pallas kernels: 125 us -> 104 us  [on_device(): pl.pallas_call(body, out_shape=jax.ShapeDtypeStruct((2, 96, WIDTH), BF16)...]
    unnamed x4 -> x1, local copies, waits for them, and re-layouts: 5.04 us -> 1.62 us
    pad x2 -> x0, local copies, waits for them, and re-layouts: 1.41 us -> none  [by_tap(): return jnp.pad(jnp.swapaxes(tails, 1, 2), ((0, 0), (0, 0), (0, 4), (0, 0)))]
where the time goes in v2:
time: 106 us
  Pallas kernels  104 us (98%)
  local copies, waits for them, and re-layouts  1.62 us (2%)
    pallas_call x1, Pallas kernels, on_device(): pl.pallas_call(body, out_shape=jax.ShapeDtypeStruct((2, 96, WIDTH), BF16)...  104 us

profile of v2, /device:TPU:1, one launch (start us, length us, event | category | flops | bytes accessed | tf_op | source)
XLA Modules:
  0.0 105.9 jit_solution(13808857705455604765)
XLA Ops:
  0.0 104.3 %shard_map.172 = bf16[2,96,512]{2,1,0:T(8,128)(2,1)} custom-call(bf16[2,96,512]{2,1,0:T(8,128)(2,1)} %emb_h.1, bf16[2,12,2048,128]{3,2,1,0:T(8,128)(2,1)} %bitcast.10, bf16[36,2,2048]{2,1,0:T(2,128)(2,1)} %bitcast.11, bf16[36,2,256]{2,1,0:T(2,128)(2,1)} %bitcast.12, s32[1,96]{1,0:T(1,128)} %bitcast.14, s32[1,96]{1,0:T(1,128)} %bitcast.15, ...), custom_call_target="tpu_custom_call" | custom-call | tf_op jit(solution)/shard_map/pallas_call | solution.py:541
  104.3 1.6 %copy.20 = bf16[2,96,512]{2,1,0:T(8,128)(2,1)} copy(bf16[2,96,512]{2,1,0:T(8,128)(2,1)} %shard_map.172) | data formatting | bytes 393216

commit v3 on v2

--- a/solution.py
+++ b/solution.py
@@ -16,7 +16,8 @@
 WIDTH = 512
 CH = 2048
 S = 2
-PART = 1152
+PART = 1024
+EXT = 256
 CAP = 12
 
 
@@ -108,6 +109,12 @@
     pick_a,
     pick_b,
     back,
+    e1s,
+    e1r,
+    e2s,
+    e2r,
+    e3s,
+    e3r,
     s1s,
     s1r,
     s2s,
@@ -116,8 +123,9 @@
     s3r,
     gat,
     held,
-    hs,
+    hx,
     hr,
+    hy,
     fin,
     load_sem,
     send_sem,
@@ -132,6 +140,9 @@
     z = req // 4
     x = req % 4
     mine = (z, x)
+    y = head // 2
+    core = head % 2
+    partner = head + 1 - 2 * core
 
     def peer(axis, k):
         if axis == 0:
@@ -141,10 +152,10 @@
     loads = []
     for l in range(L):
         row = [
+            (w_step.at[l], ws.at[l]),
+            (w_groups.at[l], wb.at[l]),
             (w_gate.at[l], wg.at[l]),
-            (w_step.at[l], ws.at[l]),
             (w_input.at[l], wi.at[l]),
-            (w_groups.at[l], wb.at[l]),
             (states.at[l], st.at[l]),
             (w_output.at[l], wo.at[l]),
         ]
@@ -169,8 +180,8 @@
     for k in (1, 2, 3):
         for axis in (0, 1):
             pl.semaphore_signal(barrier, inc=1, device_id=(peer(axis, k), head), device_id_type=MESH)
-    for k in range(1, 8):
-        pl.semaphore_signal(barrier, inc=1, device_id=(req, (head + k) % 8), device_id_type=MESH)
+    for to in (partner, (head + 2) % 8, (head + 4) % 8, (head + 6) % 8):
+        pl.semaphore_signal(barrier, inc=1, device_id=(req, to), device_id_type=MESH)
 
     for c in first:
         c.wait()
@@ -231,11 +242,11 @@
 
     place = hot(iota((16, 128), 0) == iota((16, 128), 1))
 
-    pl.semaphore_wait(barrier, 13)
+    pl.semaphore_wait(barrier, 10)
 
     def drain(l, t, phase):
-        for half in (0, 1):
-            f = flights.pop((l, t, phase, half), None)
+        for part in (0, 1, 2):
+            f = flights.pop((l, t, phase, part), None)
             if f is not None:
                 f.wait_send()
 
@@ -245,19 +256,27 @@
         )
 
     flights = {}
-    others = {}
-
-    def exchange(l, t, phase, half):
-        send, recv = ((s1s, s1r), (s2s, s2r), (s3s, s3r))[phase]
-        axis = (phase + half) % 2
+
+    def exchange(l, t, phase, part):
+        pairs = ((s1s, s1r), (s2s, s2r), (s3s, s3r)) if part < 2 else ((e1s, e1r), (e2s, e2r), (e3s, e3r))
+        send, recv = (ref.at[l, t, part] if part < 2 else ref.at[l, t] for ref in pairs[phase])
+        axis = (phase + part) % 2
         me = mine[axis]
-        e = 2 * phase + half
+        e = 3 * phase + part
         sems = (send_sem.at[t, e], recv_sem.at[t, e])
         for k in (2, 1, 3):
-            copy(send.at[l, t, half, (me + k) % 4], recv.at[l, t, half, me], *sems, (peer(axis, k), head)).start()
-        three = (send.at[l, t, half, 0:3], recv.at[l, t, half, 0:3])
-        flights[l, t, phase, half] = copy(*three, *sems, (peer(axis, 1), head))
-        others[l, t, phase, half] = [(me + k) % 4 for k in (1, 2, 3)]
+            copy(send.at[(me + k) % 4], recv.at[me], *sems, (peer(axis, k), head)).start()
+        flights[l, t, phase, part] = copy(send.at[0:3], recv.at[0:3], *sems, (peer(axis, 1), head))
+
+    def summed(l, t, phase, part):
+        pairs = ((s1s, s1r), (s2s, s2r)) if part < 2 else ((e1s, e1r), (e2s, e2r))
+        send, recv = (ref.at[l, t, part] if part < 2 else ref.at[l, t] for ref in pairs[phase])
+        me = mine[(phase + part) % 2]
+        flights[l, t, phase, part].wait_recv()
+        total = send[me].astype(F32)
+        for k in (1, 2, 3):
+            total += recv[(me + k) % 4].astype(F32)
+        return total
 
     waited = set()
 
@@ -270,9 +289,6 @@
         many = len(steps)
         x_now = jnp.concatenate([stream[t] for t in steps], axis=0)
         lhs_a = (x_now * norm_gain[l : l + 1, :]).astype(BF16)
-        lhs_b = jnp.concatenate(
-            [dot(perm_b[...], lhs_a[ROWS * i : ROWS * i + ROWS]).astype(BF16) for i in range(many)], axis=0
-        )
         squares = jnp.sum(x_now * x_now, axis=1, keepdims=True)
 
         def put(half, cols, low, high):
@@ -291,55 +307,64 @@
 
             lax.fori_loop(0, 4, tile, 0)
 
-        end = slice(1024, PART)
-        ready(l, 1)
+        ready(l, 0)
         small = dot(dot_t(lhs_a, ws[l]).astype(BF16), place)
         small = jnp.where(iota((ROWS * many, 128), 1) == 16, squares, small)
-        put(0, end, small, jnp.zeros_like(small))
-        ready(l, 0)
+        ready(l, 1)
+        bc = dot(lhs_a, wb[l])
+        low = jnp.concatenate([small, bc[:, :128]], axis=1)
+        high = jnp.concatenate([jnp.zeros_like(small), bc[:, 128:]], axis=1)
+        for i, t in enumerate(steps):
+            for g in range(4):
+                rows = slice(ROWS * i + 24 * g, ROWS * i + 24 * g + 24)
+                e1s[l, t, g] = jnp.concatenate([low[rows], high[rows]], axis=0).astype(BF16)
+            exchange(l, t, 0, 2)
+        ready(l, 2)
         main(0, lhs_a, wg)
-        for t in steps:
-            exchange(l, t, 0, 0)
+        if many == 1:
+            exchange(l, steps[0], 0, 0)
         ready(l, 3)
-        bc = dot(lhs_b, wb[l])
-        put(1, end, bc[:, :128], bc[:, 128:])
-        ready(l, 2)
+        lhs_b = jnp.concatenate(
+            [dot(perm_b[...], lhs_a[ROWS * i : ROWS * i + ROWS]).astype(BF16) for i in range(many)], axis=0
+        )
         main(1, lhs_b, wi)
         for t in steps:
+            if many > 1:
+                exchange(l, t, 0, 0)
             exchange(l, t, 0, 1)
 
-    def second(l, t):
-        for half in (0, 1):
-            flights[l, t, 0, half].wait_recv()
-            total = s1s[l, t, half, mine[half]].astype(F32)
-            for src in others[l, t, 0, half]:
-                total += s1r[l, t, half, src].astype(F32)
-            put = dot((sel_a if half == 0 else sel_b)[...], total.astype(BF16)).astype(BF16)
+    def second(l, t, parts):
+        for part in parts:
+            sel = (sel_b if part == 1 else sel_a)[...]
+            put = dot(sel, summed(l, t, 0, part).astype(BF16)).astype(BF16)
             for g in range(4):
-                s2s[l, t, half, g] = put[32 * g : 32 * g + 32]
-            exchange(l, t, 1, half)
-
-    def third(l, t):
-        for half in (0, 1):
-            flights[l, t, 1, half].wait_recv()
-            total = s2s[l, t, half, mine[1 - half]].astype(F32)
-            for src in others[l, t, 1, half]:
-                total += s2r[l, t, half, src].astype(F32)
+                if part < 2:
+                    s2s[l, t, part, g] = put[32 * g : 32 * g + 32]
+                else:
+                    e2s[l, t, g] = put[32 * g : 32 * g + 32]
+            exchange(l, t, 1, part)
+
+    def third(l, t, parts):
+        for part in parts:
+            total = summed(l, t, 1, part)
             for g in range(4):
-                s3s[l, t, half, g] = total[8 * g : 8 * g + 8]
-            exchange(l, t, 2, half)
-
-    def landed(l, t, half):
-        me = mine[half]
-        flights[l, t, 2, half].wait_recv()
-        s3r[l, t, half, me] = s3s[l, t, half, me]
-        block = s3r[l, t, half].reshape(32, PART)
-        pick = (pick_a if half == 0 else pick_b)[...]
-        high = block.astype(BF16)
-        low = (block - high.astype(F32)).astype(BF16)
-        both = dot(pick, high) + dot(pick, low)
-        main = jnp.concatenate([both[:16, :1024], both[16:, :1024]], axis=1)
-        return main, both[:16, 1024:], both[16:, 1024:]
+                if part < 2:
+                    s3s[l, t, part, g] = total[8 * g : 8 * g + 8]
+                else:
+                    e3s[l, t, g] = total[8 * g : 8 * g + 8]
+            exchange(l, t, 2, part)
+
+    def landed(l, t, part):
+        send, recv = (ref.at[l, t, part] if part < 2 else ref.at[l, t] for ref in ((s3s, s3r) if part < 2 else (e3s, e3r)))
+        me = mine[part % 2]
+        flights[l, t, 2, part].wait_recv()
+        recv[me] = send[me]
+        block = recv[...].reshape(32, recv.shape[2])
+        pick = (pick_b if part == 1 else pick_a)[...]
+        top = block.astype(BF16)
+        rest = (block - top.astype(F32)).astype(BF16)
+        both = dot(pick, top) + dot(pick, rest)
+        return both[:16], both[16:]
 
     kept = {}
 
@@ -349,53 +374,59 @@
         seq = (tail + [pre]) if old is None else (tail[1:] + [old.astype(BF16).astype(F32), pre])
         return silu(seq[0] * tap[0] + seq[1] * tap[1] + seq[2] * tap[2] + seq[3] * tap[3])
 
-    def scan(l, t):
-        xm, xb, xc = landed(l, t, 1)
-        gm, small, _ = landed(l, t, 0)
+    def early(l, t):
+        low, high = landed(l, t, 2)
+        small = low[:, :128]
         scale = lax.rsqrt(small[:, 16:17] * (1.0 / D) + EPS)
-        dt_pre = small[:, :16] * scale
-        bc_pre = jnp.concatenate([xb, xc], axis=1) * scale
-        x_pre = xm * scale
-        old = kept.get(l)
-        bc = conv(l, bc_pre, old and old[0], tail_bc, conv_grp)
+        delta = softplus(small[:, :16] * scale + bias[l : l + 1, :])
+        decay = jnp.exp(-delta * rate[l : l + 1, :])
+        bc_pre = jnp.concatenate([low[:, 128:], high[:, 128:]], axis=1) * scale
+        bc = conv(l, bc_pre, kept[l, 0][4] if t else None, tail_bc, conv_grp)
         b_now, c_now = bc[:, :128], bc[:, 128:]
-        c_low = c_now.astype(BF16)
-        slot_of = iota((16, 1), 0)
+        k_now = delta * jnp.sum(b_now * c_now, axis=1, keepdims=True) + skip[l : l + 1, :]
+        if t == 0:
+            k_state, k_old = decay, None
+        else:
+            _, delta_old, decay_old, b_old = kept[l, 0][:4]
+            k_state = decay * decay_old
+            k_old = decay * delta_old * jnp.sum(b_old * c_now, axis=1, keepdims=True)
+        kept[l, t] = (scale, delta, decay, b_now, bc_pre, k_state, k_now, k_old)
+        kept[l, t, "c"] = c_now.astype(BF16)
+
+    def contract(l):
+        both_c = jnp.concatenate([kept[l, 0, "c"], kept[l, 1, "c"]], axis=0)
+        slot_of = iota((32, 1), 0) & 15
+        zero = jnp.zeros((), BF16)
         ready(l, 4)
-        held[...] = jnp.zeros_like(held)
-
-        zero = jnp.zeros((), BF16)
-
-        def contract(i, _):
+        held[...] = jnp.zeros((32, CH), F32)
+
+        def pair_of(i, _):
             c = 2 * i
-            lhs = jnp.concatenate([jnp.where(slot_of == c, c_low, zero), jnp.where(slot_of == c + 1, c_low, zero)], axis=1)
+            lhs = jnp.concatenate([jnp.where(slot_of == c, both_c, zero), jnp.where(slot_of == c + 1, both_c, zero)], axis=1)
             for j in range(4):
                 rows = slice(512 * j, 512 * j + 512)
                 pair = jnp.concatenate([st[l, c, rows, :], st[l, c + 1, rows, :]], axis=1)
                 held[:, rows] += dot_t(lhs, pair)
             return 0
 
-        lax.fori_loop(0, CAP // 2, contract, 0)
-        delta = softplus(dt_pre + bias[l : l + 1, :])
-        decay = jnp.exp(-delta * rate[l : l + 1, :])
-        x_now = conv(l, x_pre, old and old[1], tail_x, conv_in)
-        k_now = delta * jnp.sum(b_now * c_now, axis=1, keepdims=True) + skip[l : l + 1, :]
-        if t == 0:
-            kept[l] = (bc_pre, x_pre, b_now, x_now, delta, decay)
-            k_state = decay
-        else:
-            _, _, b_old, x_old, delta_old, decay_old = old
-            k_state = decay * decay_old
-            k_old = decay * delta_old * jnp.sum(b_old * c_now, axis=1, keepdims=True)
+        lax.fori_loop(0, CAP // 2, pair_of, 0)
+
+    def scan(l, t):
+        scale, k_state, k_now, k_old = (kept[l, t][i] for i in (0, 5, 6, 7))
+        x_pre = jnp.concatenate(landed(l, t, 1), axis=1) * scale
+        x_old_pre, x_old = kept.get((l, "x"), (None, None))
+        x_now = conv(l, x_pre, x_old_pre, tail_x, conv_in)
+        kept[l, "x"] = (x_pre, x_now)
         outs = []
         for h in range(16):
             cols = slice(128 * h, 128 * h + 128)
             one = slice(h, h + 1)
-            y = k_state[:, one] * held[:, cols] + k_now[:, one] * x_now[:, cols]
+            y = k_state[:, one] * held[16 * t : 16 * t + 16, cols] + k_now[:, one] * x_now[:, cols]
             if t == 1:
                 y += k_old[:, one] * x_old[:, cols]
             outs.append(y)
-        gated = jnp.concatenate(outs, axis=1) * silu(gm * scale)
+        gate_pre = jnp.concatenate(landed(l, t, 0), axis=1) * scale
+        gated = jnp.concatenate(outs, axis=1) * silu(gate_pre)
         mean_sq = jnp.sum(gated * gated, axis=1, keepdims=True) * (1.0 / CH)
         normed = (gated * lax.rsqrt(mean_sq + EPS) * out_gain[l : l + 1, :]).astype(BF16)
         for half in (0, 1):
@@ -418,15 +449,6 @@
             flights[l, t, 3, half].wait_recv()
             gather(l, t, 1, half)
 
-    def to_heads(l, t, stage):
-        sems = (hsend_sem.at[t, stage], hrecv_sem.at[t, stage])
-        for k in (4, 3, 5, 2, 6, 1, 7):
-            to = (head + k) % 8
-            pair = (hs.at[l, t, to], hr.at[l, t, head]) if stage == 0 else (fin.at[l, t, head], fin.at[l, t, head])
-            copy(*pair, *sems, (req, to)).start()
-        seven = (hs.at[l, t, 0:7], hr.at[l, t, 0:7]) if stage == 0 else (fin.at[l, t, 0:7], fin.at[l, t, 0:7])
-        flights[l, t, 5 + stage, 0] = copy(*seven, *sems, (req, (head + 1) % 8))
-
     def output(l, t):
         ready(l, 5)
         part = None
@@ -436,29 +458,38 @@
             lhs = jnp.concatenate([dot(back[half, sub], rows).astype(BF16) for sub in range(4)], axis=1)
             more = dot(lhs, wo[l, 1024 * half : 1024 * half + 1024, :])
             part = more if part is None else part + more
-        for h in range(8):
-            i, c = h // 4, h % 4
-            hs[l, t, h] = part[48 * i : 48 * i + 48, 128 * c : 128 * c + 128].astype(BF16)
-        to_heads(l, t, 0)
+        low, high = part[:48], part[48:]
+        hx[l, t, 0] = jnp.where(core == 0, low, high)
+        hx[l, t, 1] = jnp.where(core == 0, high, low)
+        f = copy(hx.at[l, t, 1], hr.at[l, t], hsend_sem.at[l, t, 0], hrecv_sem.at[l, t, 0], (req, partner))
+        f.start()
+        flights[l, t, 5, 0] = f
 
     def reduce(l, t):
-        total = hs[l, t, head].astype(F32)
         flights[l, t, 5, 0].wait_recv()
-        for k in range(1, 8):
-            total += hr[l, t, (head + k) % 8].astype(F32)
-        fin[l, t, head] = total.astype(BF16)
-        to_heads(l, t, 1)
+        hy[l, t, y] = (hx[l, t, 0] + hr[l, t]).astype(BF16)
+        sems = (hsend_sem.at[l, t, 1], hrecv_sem.at[l, t, 1])
+        for k in (2, 1, 3):
+            copy(hy.at[l, t, y], hy.at[l, t, y], *sems, (req, (head + 2 * k) % 8)).start()
+        three = hy.at[l, t, 0:3]
+        flights[l, t, 6, 0] = copy(three, three, *sems, (req, (head + 2) % 8))
 
     def finish(l, t):
         flights[l, t, 6, 0].wait_recv()
-        for h in range(8):
-            i, c = h // 4, h % 4
-            rows, cols = slice(48 * i, 48 * i + 48), slice(128 * c, 128 * c + 128)
-            now = stream[t, rows, cols] + fin[l, t, h].astype(F32)
-            if l < L - 1:
-                stream[t, rows, cols] = now
-            else:
-                out[t, rows, cols] = now.astype(BF16)
+        total = hy[l, t, 0].astype(F32)
+        for i in (1, 2, 3):
+            total += hy[l, t, i].astype(F32)
+        fin[l, t, core] = total
+        f = copy(fin.at[l, t, core], fin.at[l, t, core], hsend_sem.at[l, t, 2], hrecv_sem.at[l, t, 2], (req, partner))
+        f.start()
+        flights[l, t, 7, 0] = f
+
+    def close(l, t):
+        flights[l, t, 7, 0].wait_recv()
+        if l < L - 1:
+            stream[t] += fin[l, t].reshape(ROWS, WIDTH)
+        else:
+            out[t] = (stream[t] + fin[l, t].reshape(ROWS, WIDTH)).astype(BF16)
 
     project(0, (0, 1))
     tables()
@@ -472,42 +503,60 @@
         for i in range(36):
             rows[2 * i : 2 * i + 2, :] = tails[i].astype(F32)
         rows[...] = dot(by_layer, rows[0:72, :].astype(BF16))
+    second(0, 0, (2,))
+    second(0, 1, (2,))
     for l in range(L):
-        second(l, 0)
-        second(l, 1)
+        last = l == L - 1
+        second(l, 0, (0, 1))
+        if l:
+            second(l, 1, (2,))
+        third(l, 0, (2,))
+        second(l, 1, (0, 1))
         if l == 0:
             for c in loads[1]:
                 c.start()
-        third(l, 0)
+        third(l, 1, (2,))
         drain(l, 0, 0)
-        third(l, 1)
         drain(l, 1, 0)
+        third(l, 0, (0, 1))
+        early(l, 0)
+        early(l, 1)
+        third(l, 1, (0, 1))
+        contract(l)
         scan(l, 0)
         scan(l, 1)
         forward(l, 0)
-        drain(l, 0, 1)
-        drain(l, 0, 2)
-        drain(l, 1, 1)
-        drain(l, 1, 2)
+        for phase in (1, 2):
+            drain(l, 0, phase)
+            drain(l, 1, phase)
         forward(l, 1)
         drain(l, 0, 3)
         drain(l, 1, 3)
         output(l, 0)
+        reduce(l, 0)
         output(l, 1)
         drain(l, 0, 4)
-        reduce(l, 0)
+        drain(l, 0, 5)
+        if last:
+            reduce(l, 1)
+            finish(l, 0)
+        else:
+            finish(l, 0)
+            reduce(l, 1)
+        close(l, 0)
+        if not last:
+            project(l + 1, (0,))
         drain(l, 1, 4)
-        reduce(l, 1)
-        drain(l, 0, 5)
-        finish(l, 0)
-        if l < L - 1:
-            project(l + 1, (0,))
         drain(l, 1, 5)
+        drain(l, 0, 6)
+        drain(l, 0, 7)
         finish(l, 1)
-        if l < L - 1:
+        close(l, 1)
+        if not last:
+            second(l + 1, 0, (2,))
             project(l + 1, (1,))
-        drain(l, 0, 6)
         drain(l, 1, 6)
+        drain(l, 1, 7)
     for key in list(flights):
         drain(*key[:3])
 
@@ -572,6 +621,12 @@
             pltpu.VMEM((32, 32), BF16),
             pltpu.VMEM((32, 32), BF16),
             pltpu.VMEM((2, 4, ROWS, 768), BF16),
+            pltpu.VMEM((L, S, 4, 48, EXT), BF16),
+            pltpu.VMEM((L, S, 4, 48, EXT), BF16),
+            pltpu.VMEM((L, S, 4, 32, EXT), BF16),
+            pltpu.VMEM((L, S, 4, 32, EXT), BF16),
+            pltpu.VMEM((L, S, 4, 8, EXT), F32),
+            pltpu.VMEM((L, S, 4, 8, EXT), F32),
             pltpu.VMEM((L, S, 2, 4, 48, PART), BF16),
             pltpu.VMEM((L, S, 2, 4, 48, PART), BF16),
             pltpu.VMEM((L, S, 2, 4, 32, PART), BF16),
@@ -579,17 +634,18 @@
             pltpu.VMEM((L, S, 2, 4, 8, PART), F32),
             pltpu.VMEM((L, S, 2, 4, 8, PART), F32),
             pltpu.VMEM((L, S, 2, 4, 4, 48, 256), BF16),
-            pltpu.VMEM((16, CH), F32),
-            pltpu.VMEM((L, S, 8, 48, 128), BF16),
-            pltpu.VMEM((L, S, 8, 48, 128), BF16),
-            pltpu.VMEM((L, S, 8, 48, 128), BF16),
+            pltpu.VMEM((32, CH), F32),
+            pltpu.VMEM((L, S, 2, 48, WIDTH), F32),
+            pltpu.VMEM((L, S, 48, WIDTH), F32),
+            pltpu.VMEM((L, S, 4, 48, WIDTH), BF16),
+            pltpu.VMEM((L, S, 2, 48, WIDTH), F32),
             pltpu.SemaphoreType.DMA((L, 6)),
-            pltpu.SemaphoreType.DMA((S, 6)),
-            pltpu.SemaphoreType.DMA((S, 6)),
+            pltpu.SemaphoreType.DMA((S, 9)),
+            pltpu.SemaphoreType.DMA((S, 9)),
             pltpu.SemaphoreType.DMA((S, 2, 2)),
             pltpu.SemaphoreType.DMA((S, 2, 2)),
-            pltpu.SemaphoreType.DMA((S, 2)),
-            pltpu.SemaphoreType.DMA((S, 2)),
+            pltpu.SemaphoreType.DMA((L, S, 3)),
+            pltpu.SemaphoreType.DMA((L, S, 3)),
         ],
         compiler_params=pltpu.CompilerParams(
             collective_id=0, has_side_effects=True, vmem_limit_bytes=58 * 2**20

time: 106 us -> 100 us (0.943)
  Pallas kernels: 104 us -> 98.6 us
    pallas_call x1, Pallas kernels: 104 us -> 98.6 us  [on_device(): pl.pallas_call(body, out_shape=jax.ShapeDtypeStruct((2, 96, WIDTH), BF16)...]
where the time goes in v3:
time: 100 us
  Pallas kernels  98.6 us (99%)
  local copies, waits for them, and re-layouts  1.62 us (2%)
    pallas_call x1, Pallas kernels, on_device(): pl.pallas_call(body, out_shape=jax.ShapeDtypeStruct((2, 96, WIDTH), BF16)...  98.6 us

profile of v3, /device:TPU:1, one launch (start us, length us, event | category | flops | bytes accessed | tf_op | source)
XLA Modules:
  0.0 100.2 jit_solution(4172746837623117925)
XLA Ops:
  0.0 98.6 %shard_map.172 = bf16[2,96,512]{2,1,0:T(8,128)(2,1)} custom-call(bf16[2,96,512]{2,1,0:T(8,128)(2,1)} %emb_h.1, bf16[2,12,2048,128]{3,2,1,0:T(8,128)(2,1)} %bitcast.10, bf16[36,2,2048]{2,1,0:T(2,128)(2,1)} %bitcast.11, bf16[36,2,256]{2,1,0:T(2,128)(2,1)} %bitcast.12, s32[1,96]{1,0:T(1,128)} %bitcast.14, s32[1,96]{1,0:T(1,128)} %bitcast.15, ...), custom_call_target="tpu_custom_call" | custom-call | tf_op jit(solution)/shard_map/pallas_call | solution.py:590
  98.6 1.6 %copy.20 = bf16[2,96,512]{2,1,0:T(8,128)(2,1)} copy(bf16[2,96,512]{2,1,0:T(8,128)(2,1)} %shard_map.172) | data formatting | bytes 393216
